TPU v7x, 32 devices: a whole 2x2x4 slice. The times are simulated.
32 devices in a mesh: seq: 8 (over y, x, core), ctx: 4 (over z).
Axes of the slice: x: 2, y: 2, z: 4, core: 2. Of those that a mesh axis runs over, the one named last changes fastest.
Arguments:
- tokens: bfloat16 [8192, 1024], P(('seq', 'ctx')), may hold values from -6 to 6
- first_values: bfloat16 [8192, 1024], P(('seq', 'ctx')), may hold values from -6 to 6
- gain_attn: bfloat16 [1024], P(('seq', 'ctx')), may hold values from 0.099609375 to 1.8984375
- w_query: bfloat16 [1024, 1024], P(('seq', 'ctx')), may hold values from -0.1875 to 0.1875
- w_key: bfloat16 [1024, 1024], P(('seq', 'ctx')), may hold values from -0.1875 to 0.1875
- w_value: bfloat16 [1024, 1024], P(('seq', 'ctx')), may hold values from -0.1875 to 0.1875
- w_out: bfloat16 [1024, 1024], P(('seq', 'ctx')), may hold values from -2 to 2
- gain_ffn: bfloat16 [1024], P(('seq', 'ctx')), may hold values from 0.099609375 to 1.8984375
- w_gate: bfloat16 [1024, 2816], P(('seq', 'ctx')), may hold values from -0.1875 to 0.1875
- w_up: bfloat16 [1024, 2816], P(('seq', 'ctx')), may hold values from -0.1875 to 0.1875
- w_down: bfloat16 [2816, 1024], P(('seq', 'ctx')), may hold values from -0.109375 to 0.109375
- segment_start: int32 [8192], P(('seq', 'ctx')), may hold values from 0 to 1023, as said below
- cotangent: bfloat16 [8192, 1024], P(('seq', 'ctx')), may hold values from -6 to 6
Outputs:
- block_out: bfloat16 [8192, 1024], P(('seq', 'ctx'))
- grad_tokens: bfloat16 [8192, 1024], P(('seq', 'ctx'))
- grad_first_values: bfloat16 [8192, 1024], P(('seq', 'ctx'))
- grad_gain_attn: float32 [1024], P(('seq', 'ctx'))
- grad_w_query: float32 [1024, 1024], P(('seq', 'ctx'))
- grad_w_key: float32 [1024, 1024], P(('seq', 'ctx'))
- grad_w_value: float32 [1024, 1024], P(('seq', 'ctx'))
- grad_w_out: float32 [1024, 1024], P(('seq', 'ctx'))
- grad_gain_ffn: float32 [1024], P(('seq', 'ctx'))
- grad_w_gate: float32 [1024, 2816], P(('seq', 'ctx'))
- grad_w_up: float32 [1024, 2816], P(('seq', 'ctx'))
- grad_w_down: float32 [2816, 1024], P(('seq', 'ctx'))
Inputs may be any that keep to these rules, and one draw needn't show every extreme that they name: `segment_start`: documents are runs of consecutive tokens inside one sequence; each token holds the place of its document's first token. In every sequence one document begins within the first 128 tokens and ends within the last 128, and the last token of every sequence begins a document of its own.
All inputs are finite; a program needn't handle non-finite values.
Results may differ from a plain program's by a relative error of at most 0.03.
Values may be sent and summed in bfloat16 or wider, within the bound.
A program may use at most 256 MiB of HBM per device.

v0:
```python
import jax
import jax.numpy as jnp
from jax import lax
from jax.sharding import PartitionSpec as P

HEADS = 16
HD = 64


norm_eps = 1e-06
masked_score = -2e30
start_score = -1e30


def rms_scale(features, scale_gain):
    return (
        features
        * lax.rsqrt(jnp.mean(features * features, axis=-1, keepdims=True) + norm_eps)
        * scale_gain
    )


def rope_angles(positions, head_size):
    half_size = head_size // 2
    frequency = 10000.0 ** (-(jnp.arange(half_size, dtype=jnp.float32) * 2.0) / head_size)
    angles = positions.astype(jnp.float32)[:, None] * frequency[None, :]
    return jnp.concatenate([angles, angles], axis=-1)


def rotate(features, angles):
    half_size = features.shape[-1] // 2
    turned = jnp.concatenate([-features[..., half_size:], features[..., :half_size]], axis=-1)
    return features * jnp.cos(angles)[:, None, :] + turned * jnp.sin(angles)[:, None, :]


def block_size(shard_rows):
    size_guess = shard_rows * max(1, 640 // shard_rows)
    return size_guess


def masked_scores(queries, keys_part, query_index, query_start, key_index, key_start, score_scale):
    scores = (
        jnp.einsum("qhd,khd->hqk", queries, keys_part, preferred_element_type=jnp.float32)
        * score_scale
    )
    allowed = (query_start[:, None] == key_start[None, :]) & (
        key_index[None, :] <= query_index[:, None]
    )
    return jnp.where(allowed[None], scores, masked_score)


def per_device(
    tokens,
    first_values,
    gain_attn,
    w_query,
    w_key,
    w_value,
    w_out,
    gain_ffn,
    w_gate,
    w_up,
    w_down,
    segment_start,
    cotangent,
):
    tok_rows, model_width = tokens.shape
    score_scale = HD ** (-0.5)
    own_weights = (gain_attn, w_query, w_key, w_value, w_out, gain_ffn, w_gate, w_up, w_down)
    full_weights = (
        lax.all_gather(own_weights[0], ("seq", "ctx"), axis=0, tiled=True),
        lax.all_gather(own_weights[1], ("seq", "ctx"), axis=0, tiled=True),
        lax.all_gather(own_weights[2], ("seq", "ctx"), axis=0, tiled=True),
        lax.all_gather(own_weights[3], ("seq", "ctx"), axis=0, tiled=True),
        lax.all_gather(own_weights[4], ("seq", "ctx"), axis=0, tiled=True),
        lax.all_gather(own_weights[5], ("seq", "ctx"), axis=0, tiled=True),
        lax.all_gather(own_weights[6], ("seq", "ctx"), axis=0, tiled=True),
        lax.all_gather(own_weights[7], ("seq", "ctx"), axis=0, tiled=True),
        lax.all_gather(own_weights[8], ("seq", "ctx"), axis=0, tiled=True),
    )
    all_starts = lax.all_gather(segment_start, "ctx", axis=0, tiled=True)
    own_index = lax.axis_index("ctx") * tok_rows + jnp.arange(tok_rows, dtype=jnp.int32)
    angles = rope_angles(own_index - segment_start, HD)
    (
        gain_one,
        query_weight,
        key_weight,
        value_weight,
        out_weight,
        gain_two,
        gate_weight,
        up_weight,
        down_weight,
    ) = full_weights
    token_float = tokens.astype(jnp.float32)
    normed = rms_scale(token_float, gain_one.astype(jnp.float32)).astype(jnp.bfloat16)
    query_raw = jnp.dot(normed, query_weight, preferred_element_type=jnp.float32).reshape(
        tok_rows, HEADS, HD
    )
    key_raw = jnp.dot(normed, key_weight, preferred_element_type=jnp.float32).reshape(
        tok_rows, HEADS, HD
    )
    queries = rotate(query_raw, angles).astype(jnp.bfloat16)
    keys_rot = rotate(key_raw, angles).astype(jnp.bfloat16)
    values = (
        0.5 * jnp.dot(normed, value_weight, preferred_element_type=jnp.float32)
        + 0.5 * first_values.astype(jnp.float32)
    ).astype(jnp.bfloat16)
    values_heads = values.reshape(tok_rows, HEADS, HD)
    keys_flat = keys_rot.reshape(tok_rows, model_width)
    forward_init = (
        jnp.full((HEADS, tok_rows), start_score, jnp.float32),
        jnp.zeros((HEADS, tok_rows), jnp.float32),
        jnp.zeros((HEADS, tok_rows, HD), jnp.float32),
    )
    running = forward_init
    key_piece = lax.all_gather(keys_flat, "ctx", axis=0, tiled=True)
    value_piece = lax.all_gather(values, "ctx", axis=0, tiled=True)
    piece_rows = key_piece.shape[0]
    size_now = block_size(tok_rows)
    block_count = piece_rows // size_now
    key_blocks = key_piece.reshape(block_count, size_now, HEADS, HD)
    value_blocks = value_piece.reshape(block_count, size_now, HEADS, HD)
    block_starts = jnp.arange(block_count, dtype=jnp.int32) * size_now

    def forward_one_block(partial_value, inputs):
        key_block, value_block, block_start = inputs
        key_index = block_start + jnp.arange(size_now, dtype=jnp.int32)
        key_start = lax.dynamic_slice_in_dim(all_starts, block_start, size_now)
        run_max, run_sum, accum_out = partial_value
        scores = masked_scores(
            queries, key_block, own_index, segment_start, key_index, key_start, score_scale
        )
        new_max = jnp.maximum(run_max, jnp.max(scores, axis=-1))
        weights = jnp.exp(scores - new_max[..., None])
        factor = jnp.exp(run_max - new_max)
        new_sum = run_sum * factor + jnp.sum(weights, axis=-1)
        new_accum = accum_out * factor[..., None] + jnp.einsum(
            "hqk,khd->hqd",
            weights.astype(jnp.bfloat16),
            value_block,
            preferred_element_type=jnp.float32,
        )
        partial_value = (new_max, new_sum, new_accum)
        return (partial_value, None)

    running, _ = lax.scan(forward_one_block, running, (key_blocks, value_blocks, block_starts))
    run_max, run_sum, accum_out = running
    attn_heads = accum_out / run_sum[..., None]
    log_total = run_max + jnp.log(run_sum)
    attn_low = attn_heads.transpose(1, 0, 2).reshape(tok_rows, model_width).astype(jnp.bfloat16)
    resid = token_float + jnp.dot(attn_low, out_weight, preferred_element_type=jnp.float32)
    normed_two = rms_scale(resid, gain_two.astype(jnp.float32)).astype(jnp.bfloat16)
    gate = jnp.dot(normed_two, gate_weight, preferred_element_type=jnp.float32)
    up_proj = jnp.dot(normed_two, up_weight, preferred_element_type=jnp.float32)
    hidden = (jax.nn.silu(gate) * up_proj).astype(jnp.bfloat16)
    block_out = (resid + jnp.dot(hidden, down_weight, preferred_element_type=jnp.float32)).astype(
        jnp.bfloat16
    )
    grad_down = jnp.einsum("tf,td->fd", hidden, cotangent, preferred_element_type=jnp.float32)
    d_hidden = jnp.einsum("td,fd->tf", cotangent, down_weight, preferred_element_type=jnp.float32)
    silu_value, silu_back = jax.vjp(jax.nn.silu, gate)
    d_gate = silu_back(d_hidden * up_proj)[0].astype(jnp.bfloat16)
    d_up = (d_hidden * silu_value).astype(jnp.bfloat16)
    grad_gate = jnp.einsum("td,tf->df", normed_two, d_gate, preferred_element_type=jnp.float32)
    grad_up = jnp.einsum("td,tf->df", normed_two, d_up, preferred_element_type=jnp.float32)
    d_normed_two = jnp.einsum(
        "tf,df->td", d_gate, gate_weight, preferred_element_type=jnp.float32
    ) + jnp.einsum("tf,df->td", d_up, up_weight, preferred_element_type=jnp.float32)
    _, norm_two_back = jax.vjp(rms_scale, resid, gain_two.astype(jnp.float32))
    resid_part, grad_gain_two = norm_two_back(d_normed_two)
    d_resid = cotangent.astype(jnp.float32) + resid_part
    d_branch = d_resid.astype(jnp.bfloat16)
    grad_out = jnp.einsum("td,te->de", attn_low, d_branch, preferred_element_type=jnp.float32)
    d_attn = jnp.einsum(
        "te,de->td", d_branch, out_weight, preferred_element_type=jnp.float32
    ).astype(jnp.bfloat16)
    d_attn_heads = d_attn.reshape(tok_rows, HEADS, HD)
    delta_heads = jnp.sum(d_attn_heads.astype(jnp.float32).transpose(1, 0, 2) * attn_heads, axis=-1)
    all_log_total, all_delta = (
        lax.all_gather(log_total.T.astype(jnp.bfloat16), "ctx", axis=0, tiled=True).astype(
            jnp.float32
        ),
        lax.all_gather(delta_heads.T.astype(jnp.bfloat16), "ctx", axis=0, tiled=True).astype(
            jnp.float32
        ),
    )
    d_query_sum = jnp.zeros((tok_rows, HEADS, HD), jnp.float32)
    key_piece = lax.all_gather(keys_flat, "ctx", axis=0, tiled=True)
    value_piece = lax.all_gather(values, "ctx", axis=0, tiled=True)
    piece_rows = key_piece.shape[0]
    query_size_now = block_size(tok_rows)
    block_count = piece_rows // query_size_now
    key_blocks = key_piece.reshape(block_count, query_size_now, HEADS, HD)
    value_blocks = value_piece.reshape(block_count, query_size_now, HEADS, HD)
    block_starts = jnp.arange(block_count, dtype=jnp.int32) * query_size_now

    def query_one_block(partial_value, inputs):
        key_block, value_block, block_start = inputs
        key_index = block_start + jnp.arange(query_size_now, dtype=jnp.int32)
        key_start = lax.dynamic_slice_in_dim(all_starts, block_start, query_size_now)
        scores = masked_scores(
            queries, key_block, own_index, segment_start, key_index, key_start, score_scale
        )
        probability = jnp.exp(scores - log_total[..., None])
        d_prob = jnp.einsum(
            "qhd,khd->hqk", d_attn_heads, value_block, preferred_element_type=jnp.float32
        )
        d_score = (probability * (d_prob - delta_heads[..., None])).astype(jnp.bfloat16)
        partial_value = (
            partial_value
            + jnp.einsum("hqk,khd->qhd", d_score, key_block, preferred_element_type=jnp.float32)
            * score_scale
        )
        return (partial_value, None)

    d_query_sum, _ = lax.scan(
        query_one_block, d_query_sum, (key_blocks, value_blocks, block_starts)
    )
    queries_flat = queries.reshape(tok_rows, model_width)
    key_init = (
        jnp.zeros((tok_rows, HEADS, HD), jnp.float32),
        jnp.zeros((tok_rows, HEADS, HD), jnp.float32),
    )
    sums_now = key_init
    query_piece = lax.all_gather(queries_flat, "ctx", axis=0, tiled=True)
    grad_piece = lax.all_gather(d_attn, "ctx", axis=0, tiled=True)
    piece_rows = query_piece.shape[0]
    key_size_now = block_size(tok_rows)
    block_count = piece_rows // key_size_now
    query_blocks = query_piece.reshape(block_count, key_size_now, HEADS, HD)
    grad_blocks = grad_piece.reshape(block_count, key_size_now, HEADS, HD)
    block_starts = jnp.arange(block_count, dtype=jnp.int32) * key_size_now

    def key_one_block(partial_value, inputs):
        query_block, grad_block, block_start = inputs
        query_index = block_start + jnp.arange(key_size_now, dtype=jnp.int32)
        query_start = lax.dynamic_slice_in_dim(all_starts, block_start, key_size_now)
        block_total = lax.dynamic_slice_in_dim(all_log_total, block_start, key_size_now).T
        block_delta = lax.dynamic_slice_in_dim(all_delta, block_start, key_size_now).T
        d_key_sum, d_value_sum = partial_value
        scores = masked_scores(
            query_block, keys_rot, query_index, query_start, own_index, segment_start, score_scale
        )
        probability = jnp.exp(scores - block_total[..., None])
        d_prob = jnp.einsum(
            "qhd,khd->hqk", grad_block, values_heads, preferred_element_type=jnp.float32
        )
        d_score = (probability * (d_prob - block_delta[..., None])).astype(jnp.bfloat16)
        d_value_sum = d_value_sum + jnp.einsum(
            "hqk,qhd->khd",
            probability.astype(jnp.bfloat16),
            grad_block,
            preferred_element_type=jnp.float32,
        )
        d_key_sum = (
            d_key_sum
            + jnp.einsum("hqk,qhd->khd", d_score, query_block, preferred_element_type=jnp.float32)
            * score_scale
        )
        partial_value = (d_key_sum, d_value_sum)
        return (partial_value, None)

    sums_now, _ = lax.scan(key_one_block, sums_now, (query_blocks, grad_blocks, block_starts))
    d_key_rot, d_values = sums_now

    def rotate_here(features):
        return rotate(features, angles)

    _, rotate_back = jax.vjp(rotate_here, query_raw)
    d_query = (
        rotate_back(d_query_sum.astype(jnp.bfloat16).astype(jnp.float32))[0]
        .astype(jnp.bfloat16)
        .reshape(tok_rows, model_width)
    )
    d_key = (
        rotate_back(d_key_rot.astype(jnp.bfloat16).astype(jnp.float32))[0]
        .astype(jnp.bfloat16)
        .reshape(tok_rows, model_width)
    )
    d_values_low = d_values.astype(jnp.bfloat16).reshape(tok_rows, model_width)
    grad_first = (0.5 * d_values_low.astype(jnp.float32)).astype(jnp.bfloat16)
    grad_query = jnp.einsum("td,te->de", normed, d_query, preferred_element_type=jnp.float32)
    grad_key = jnp.einsum("td,te->de", normed, d_key, preferred_element_type=jnp.float32)
    grad_value = jnp.einsum("td,te->de", normed, grad_first, preferred_element_type=jnp.float32)
    d_normed = jnp.einsum("te,de->td", d_query, query_weight, preferred_element_type=jnp.float32)
    d_normed = d_normed + jnp.einsum(
        "te,de->td", d_key, key_weight, preferred_element_type=jnp.float32
    )
    d_normed = d_normed + jnp.einsum(
        "te,de->td", grad_first, value_weight, preferred_element_type=jnp.float32
    )
    _, norm_one_back = jax.vjp(rms_scale, token_float, gain_one.astype(jnp.float32))
    token_part, grad_gain_one = norm_one_back(d_normed)
    grad_tokens = (d_resid + token_part).astype(jnp.bfloat16)
    reduced = (
        lax.psum_scatter(grad_gain_one, ("seq", "ctx"), scatter_dimension=0, tiled=True),
        lax.psum_scatter(grad_query, ("seq", "ctx"), scatter_dimension=0, tiled=True),
        lax.psum_scatter(grad_key, ("seq", "ctx"), scatter_dimension=0, tiled=True),
        lax.psum_scatter(grad_value, ("seq", "ctx"), scatter_dimension=0, tiled=True),
        lax.psum_scatter(grad_out, ("seq", "ctx"), scatter_dimension=0, tiled=True),
        lax.psum_scatter(grad_gain_two, ("seq", "ctx"), scatter_dimension=0, tiled=True),
        lax.psum_scatter(grad_gate, ("seq", "ctx"), scatter_dimension=0, tiled=True),
        lax.psum_scatter(grad_up, ("seq", "ctx"), scatter_dimension=0, tiled=True),
        lax.psum_scatter(grad_down, ("seq", "ctx"), scatter_dimension=0, tiled=True),
    )
    return (
        block_out,
        grad_tokens,
        grad_first,
        reduced[0],
        reduced[1],
        reduced[2],
        reduced[3],
        reduced[4],
        reduced[5],
        reduced[6],
        reduced[7],
        reduced[8],
    )


def solution(mesh):
    return jax.shard_map(
        per_device,
        mesh=mesh,
        in_specs=(
            P(("seq", "ctx"), None),
            P(("seq", "ctx"), None),
            P(("seq", "ctx")),
            P(("seq", "ctx"), None),
            P(("seq", "ctx"), None),
            P(("seq", "ctx"), None),
            P(("seq", "ctx"), None),
            P(("seq", "ctx")),
            P(("seq", "ctx"), None),
            P(("seq", "ctx"), None),
            P(("seq", "ctx"), None),
            P(("seq", "ctx")),
            P(("seq", "ctx"), None),
        ),
        out_specs=(
            P(("seq", "ctx"), None),
            P(("seq", "ctx"), None),
            P(("seq", "ctx"), None),
            P(("seq", "ctx")),
            P(("seq", "ctx"), None),
            P(("seq", "ctx"), None),
            P(("seq", "ctx"), None),
            P(("seq", "ctx"), None),
            P(("seq", "ctx")),
            P(("seq", "ctx"), None),
            P(("seq", "ctx"), None),
            P(("seq", "ctx"), None),
        ),
        check_vma=False,
    )
```

profile of v0, /device:TPU:0, one launch (start us, length us, event | category | flops | bytes accessed | tf_op | source)
XLA Modules:
  0.0 1998.0 jit_solution(13218857425254154143)
XLA Ops:
  11.2 42.0 %all-reduce.9 = (bf16[1024]{0:T(1024)(128)(2,1)S(1)}, bf16[1024]{0:T(1024)(128)(2,1)S(1)}) all-reduce(bf16[1024]{0:T(1024)(128)(2,1)S(1)} %dynamic-update-slice, bf16[1024]{0:T(1024)(128)(2,1)S(1)} %dynamic-update-slice.1), channel_id=1, replica_groups=mesh['seq'=8,'ctx'=4] {'seq','ctx'}, use_global_device_ids=true, to_apply=%add.4 | all-reduce | flops 2048 | bytes 8192
  57.4 13.0 all-gather.17.cloned.1.call-done
  73.0 55.6 %all-gather.13.cloned.1.call-done = bf16[1024,1024]{1,0:T(8,128)(2,1)} async-done(((bf16[32,1024]{1,0:T(8,128)(2,1)}), bf16[1024,1024]{1,0:T(8,128)(2,1)}) %all-gather.13.cloned.1.call-update) | async-done | bytes 2097168 | tf_op jit(solution)/shard_map/all_gather | solution.py:73
  144.2 42.7 %all-gather.19.cloned.1.call-done = bf16[1024,1024]{1,0:T(8,128)(2,1)} async-done(((bf16[32,1024]{1,0:T(8,128)(2,1)}), bf16[1024,1024]{1,0:T(8,128)(2,1)}) %all-gather.19.cloned.1.call-update) | async-done | bytes 2097168 | tf_op jit(solution)/shard_map/all_gather | solution.py:74
  193.1 9.8 all-gather
  203.3 30.5 %all-gather.15.cloned.1.call-done = bf16[1024,1024]{1,0:T(8,128)(2,1)} async-done(((bf16[256,1024]{1,0:T(8,128)(2,1)}), bf16[1024,1024]{1,0:T(8,128)(2,1)}) %all-gather.15.cloned.1.call-update) | async-done | bytes 2097168 | tf_op jit(solution)/shard_map/all_gather | solution.py:117
  244.6 35.3 %all-gather.21.cloned.1.call-done = bf16[1024,1024]{1,0:T(8,128)(2,1)} async-done(((bf16[256,1024]{1,0:T(8,128)(2,1)}), bf16[1024,1024]{1,0:T(8,128)(2,1)}) %all-gather.21.cloned.1.call-update) | async-done | bytes 2097168 | tf_op jit(solution)/shard_map/all_gather | solution.py:118
  291.7 37.9 %while.39 = (s32[]{:T(128)}, f32[16,256]{1,0:T(8,128)S(1)}, f32[16,256]{1,0:T(8,128)S(1)}, f32[16,256,64]{1,2,0:T(8,128)}, s32[256]{0:T(256)S(1)}, /*index=5*/s3...) while((s32[]{:T(128)}, f32[16,256]{1,0:T(8,128)S(1)}, ...), condition=%wide.region_4.5_spmd.clone, body=%wide.region_1.4_spmd.clone.sunk | while | flops 561140480 | bytes 64238836 | solution.py:147
  342.4 64.5 %all-gather.25.cloned.1.call-done = bf16[1024,2816]{1,0:T(8,128)(2,1)} async-done(((bf16[32,2816]{1,0:T(8,128)(2,1)}), bf16[1024,2816]{1,0:T(8,128)(2,1)}) %all-gather.25.cloned.1.call-update) | async-done | bytes 5767184 | tf_op jit(solution)/shard_map/all_gather | solution.py:77
  412.9 63.1 %all-gather.27.cloned.1.call-done = bf16[1024,2816]{1,0:T(8,128)(2,1)} async-done(((bf16[32,2816]{1,0:T(8,128)(2,1)}), bf16[1024,2816]{1,0:T(8,128)(2,1)}) %all-gather.27.cloned.1.call-update) | async-done | bytes 5767184 | tf_op jit(solution)/shard_map/all_gather | solution.py:78
  482.1 63.1 %all-gather.29.cloned.1.call-done = bf16[2816,1024]{1,0:T(8,128)(2,1)} async-done(((bf16[88,1024]{1,0:T(8,128)(2,1)}), bf16[2816,1024]{1,0:T(8,128)(2,1)}) %all-gather.29.cloned.1.call-update) | async-done | bytes 5767184 | tf_op jit(solution)/shard_map/all_gather | solution.py:79
  545.2 8.3 multiply_convert_fusion.8
  566.8 25.3 %all-gather.31.cloned.1.call-done = bf16[1024,1024]{1,0:T(8,128)(2,1)} async-done(((bf16[256,1024]{1,0:T(8,128)(2,1)}), bf16[1024,1024]{1,0:T(8,128)(2,1)}) %all-gather.31.cloned.1.call-update) | async-done | bytes 2097168 | tf_op jit(solution)/shard_map/all_gather | solution.py:226
  604.0 13.6 all_gather.63
  621.2 13.3 all_gather.65
  638.7 32.8 %while.40 = (s32[]{:T(128)}, f32[256,16,64]{0,2,1:T(8,128)}, bf16[2,512,16,64]{1,3,2,0:T(8,128)(2,1)S(1)}, s32[256]{0:T(256)S(1)}, s32[2]{0:T(128)S(1)}, /*index...) while((s32[]{:T(128)}, f32[256,16,64]{0,2,1:T(8,128)}, ...), condition=%wide.region_9.10_spmd.clone, body=%wide.region_8.9_spmd.clone.sunk | while | flops 819069696 | bytes 23378652 | solution.py:217
  646.8 8.2 fusion.221
  663.0 8.4 fusion.221
  671.5 6.4 reshape.371
  683.5 46.1 %while.41 = (s32[]{:T(128)}, f32[256,16,64]{0,2,1:T(8,128)}, f32[256,16,64]{0,2,1:T(8,128)}, bf16[2,512,16,64]{1,3,2,0:T(8,128)(2,1)S(1)}, s32[2]{0:T(128)S(1)},...) while((s32[]{:T(128)}, f32[256,16,64]{0,2,1:T(8,128)}, ...), condition=%wide.region_11.12_spmd.clone, body=%wide.region_10.11_spmd.clone.sunk | while | flops 1096418048 | bytes 35240684 | solution.py:264
  691.9 8.5 fusion.230
  714.6 8.8 fusion.230
  741.5 7.3 fusion.140
  749.2 7.3 fusion.141
  757.6 7.2 fusion.142
  776.9 39.1 %all-reduce.8 = (f32[1024]{0:T(1024)S(1)}, f32[1024]{0:T(1024)S(1)}) all-reduce(f32[1024]{0:T(1024)S(1)} %get-tuple-element.467, f32[1024]{0:T(1024)S(1)} %copy-done.33), channel_id=2, replica_groups=mesh['seq'=8,'ctx'=4] {'seq','ctx'}, use_global_device_ids=true, to_apply=%region_14.15.clone | all-reduce | flops 2048 | bytes 16384
  818.3 119.5 %reduce-scatter.8.cloned.1.call-done = f32[32,1024]{1,0:T(8,128)} async-done(((f32[1024,1024]{1,0:T(8,128)}), f32[32,1024]{1,0:T(8,128)}) %reduce-scatter.8.cloned.1.call-update) | async-done | bytes 131088 | tf_op jit(solution)/shard_map/reduce_scatter | solution.py:298
  937.8 149.3 %reduce-scatter.10.cloned.1.call-done = f32[32,1024]{1,0:T(8,128)} async-done(((f32[1024,1024]{1,0:T(8,128)}), f32[32,1024]{1,0:T(8,128)}) %reduce-scatter.10.cloned.1.call-update) | async-done | bytes 131088 | tf_op jit(solution)/shard_map/reduce_scatter | solution.py:299
  1087.1 148.7 %reduce-scatter.12.cloned.1.call-done = f32[32,1024]{1,0:T(8,128)} async-done(((f32[1024,1024]{1,0:T(8,128)}), f32[32,1024]{1,0:T(8,128)}) %reduce-scatter.12.cloned.1.call-update) | async-done | bytes 131088 | tf_op jit(solution)/shard_map/reduce_scatter | solution.py:300
  1235.8 252.7 %reduce-scatter.16.cloned.1.call-done = f32[32,2816]{1,0:T(8,128)} async-done(((f32[1024,2816]{1,0:T(8,128)}), f32[32,2816]{1,0:T(8,128)}) %reduce-scatter.16.cloned.1.call-update) | async-done | bytes 360464 | tf_op jit(solution)/shard_map/reduce_scatter | solution.py:303
  1488.5 251.2 %reduce-scatter.18.cloned.1.call-done = f32[32,2816]{1,0:T(8,128)} async-done(((f32[1024,2816]{1,0:T(8,128)}), f32[32,2816]{1,0:T(8,128)}) %reduce-scatter.18.cloned.1.call-update) | async-done | bytes 360464 | tf_op jit(solution)/shard_map/reduce_scatter | solution.py:304
  1739.7 251.2 %reduce-scatter.20.cloned.1.call-done = f32[88,1024]{1,0:T(8,128)} async-done(((f32[2816,1024]{1,0:T(8,128)}), f32[88,1024]{1,0:T(8,128)}) %reduce-scatter.20.cloned.1.call-update) | async-done | bytes 360464 | tf_op jit(solution)/shard_map/reduce_scatter | solution.py:305
  (235 shorter events, 216.5 us)
Async XLA Ops:
  7.2 63.1 %copy-start.1 = (bf16[256,1024]{1,0:T(8,128)(2,1)S(1)}, bf16[256,1024]{1,0:T(8,128)(2,1)}, u32[]{:S(2)}) copy-start(bf16[256,1024]{1,0:T(8,128)(2,1)} %param.19) | copy-start | bytes 1572868
  7.2 63.1 %all-gather.17.cloned.1.call-start = ((), (), s32[]{:S(2)}) async-start(), calls=%async_computation.9 | async-start | bytes 2162688 | tf_op jit(solution)/shard_map/all_gather | solution.py:72
  7.9 120.7 %all-gather.13.cloned.1.call-start = ((), (), s32[]{:S(2)}) async-start(), calls=%async_computation.7 | async-start | bytes 2162688 | tf_op jit(solution)/shard_map/all_gather | solution.py:73
  8.7 178.2 %all-gather.19.cloned.1.call-start = ((), (), s32[]{:S(2)}) async-start(), calls=%async_computation.10 | async-start | bytes 2162688 | tf_op jit(solution)/shard_map/all_gather | solution.py:74
  9.4 224.3 %all-gather.15.cloned.1.call-start = ((), (), s32[]{:S(2)}) async-start(), calls=%async_computation.8 | async-start | bytes 2621440 | tf_op jit(solution)/shard_map/all_gather | solution.py:117
  53.2 133.7 %copy-start.26 = (f32[1024]{0:T(1024)}, f32[1024]{0:T(1024)S(1)}, u32[]{:S(2)}) copy-start(f32[1024]{0:T(1024)S(1)} %convert_element_type.134) | copy-start | bytes 12292
  54.1 79.6 %copy-start.22 = (f32[256,64]{0,1:T(8,128)}, f32[256,64]{0,1:T(8,128)S(1)}, u32[]{:S(2)}) copy-start(f32[256,64]{0,1:T(8,128)S(1)} %get-tuple-element.577) | copy-start | bytes 196612
  54.1 79.6 %copy-start.24 = (f32[256,64]{0,1:T(8,128)}, f32[256,64]{0,1:T(8,128)S(1)}, u32[]{:S(2)}) copy-start(f32[256,64]{0,1:T(8,128)S(1)} %get-tuple-element.576) | copy-start | bytes 196612
  57.4 129.5 %copy-start.29 = (f32[256]{0:T(256)}, f32[256]{0:T(256)S(1)}, u32[]{:S(2)}) copy-start(f32[256]{0:T(256)S(1)} %fusion.121) | copy-start | bytes 3076
  72.7 55.9 %copy-start.9 = (f32[256,1024]{1,0:T(8,128)}, f32[256,1024]{1,0:T(8,128)S(1)}, u32[]{:S(2)}) copy-start(f32[256,1024]{1,0:T(8,128)S(1)} %fusion.130) | copy-start | bytes 3145732
  144.1 49.0 %copy-start.28 = (s32[256]{0:T(256)S(1)}, s32[256]{0:T(256)}, u32[]{:S(2)}) copy-start(s32[256]{0:T(256)} %param.30) | copy-start | bytes 3076
  144.1 135.7 %all-gather.21.cloned.1.call-start = ((), (), s32[]{:S(2)}) async-start(), calls=%async_computation.11 | async-start | bytes 2621440 | tf_op jit(solution)/shard_map/all_gather | solution.py:118
  190.2 147.7 %all-gather.23.cloned.1.call-start = ((), (), s32[]{:S(2)}) async-start(), calls=%async_computation.12 | async-start | bytes 2162688 | tf_op jit(solution)/shard_map/all_gather | solution.py:75
  190.8 216.1 %all-gather.25.cloned.1.call-start = ((), (), s32[]{:S(2)}) async-start(), calls=%async_computation.13 | async-start | bytes 5947392 | tf_op jit(solution)/shard_map/all_gather | solution.py:77
  191.5 284.5 %all-gather.27.cloned.1.call-start = ((), (), s32[]{:S(2)}) async-start(), calls=%async_computation.14 | async-start | bytes 5947392 | tf_op jit(solution)/shard_map/all_gather | solution.py:78
  192.3 353.0 %all-gather.29.cloned.1.call-start = ((), (), s32[]{:S(2)}) async-start(), calls=%async_computation.15 | async-start | bytes 5947392 | tf_op jit(solution)/shard_map/all_gather | solution.py:79
  193.0 399.1 %all-gather.31.cloned.1.call-start = ((), (), s32[]{:S(2)}) async-start(), calls=%async_computation.16 | async-start | bytes 2621440 | tf_op jit(solution)/shard_map/all_gather | solution.py:226
  202.9 468.6 %all-gather.33.cloned.1.call-start = ((), (), s32[]{:S(2)}) async-start(), calls=%async_computation.17 | async-start | bytes 2621440 | tf_op jit(solution)/shard_map/all_gather | solution.py:227
  300.0 5.8 copy-start
  318.4 6.1 copy-start
  553.6 5.7 copy-start.34
  564.7 253.6 %reduce-scatter.14.cloned.1.call-start = ((), (), s32[]{:S(2)}) async-start(), calls=%async_computation.21 | async-start | bytes 4325376 | tf_op jit(solution)/shard_map/reduce_scatter | solution.py:301
  638.6 299.2 %reduce-scatter.8.cloned.1.call-start = ((), (), s32[]{:S(2)}) async-start(), calls=%async_computation.18 | async-start | bytes 4325376 | tf_op jit(solution)/shard_map/reduce_scatter | solution.py:298
  677.8 5.6 copy-start.3
  683.5 46.1 %copy-start.25 = (f32[256,64]{0,1:T(8,128)S(1)}, f32[256,64]{0,1:T(8,128)}, u32[]{:S(2)}) copy-start(f32[256,64]{0,1:T(8,128)} %copy-done.24) | copy-start | bytes 196612
  735.7 351.4 %reduce-scatter.10.cloned.1.call-start = ((), (), s32[]{:S(2)}) async-start(), calls=%async_computation.19 | async-start | bytes 4325376 | tf_op jit(solution)/shard_map/reduce_scatter | solution.py:299
  738.6 497.3 %reduce-scatter.12.cloned.1.call-start = ((), (), s32[]{:S(2)}) async-start(), calls=%async_computation.20 | async-start | bytes 4325376 | tf_op jit(solution)/shard_map/reduce_scatter | solution.py:300
  741.5 747.0 %reduce-scatter.16.cloned.1.call-start = ((), (), s32[]{:S(2)}) async-start(), calls=%async_computation.22 | async-start | bytes 11894784 | tf_op jit(solution)/shard_map/reduce_scatter | solution.py:303
  748.9 990.8 %reduce-scatter.18.cloned.1.call-start = ((), (), s32[]{:S(2)}) async-start(), calls=%async_computation.23 | async-start | bytes 11894784 | tf_op jit(solution)/shard_map/reduce_scatter | solution.py:304
  756.6 1234.3 %reduce-scatter.20.cloned.1.call-start = ((), (), s32[]{:S(2)}) async-start(), calls=%async_computation.24 | async-start | bytes 11894784 | tf_op jit(solution)/shard_map/reduce_scatter | solution.py:305
  775.1 42.1 %copy-start.32 = (f32[256]{0:T(256)S(1)}, f32[256]{0:T(256)}, u32[]{:S(2)}) copy-start(f32[256]{0:T(256)} %copy-done.31) | copy-start | bytes 3076
  775.1 42.1 %copy-start.5 = (f32[256,1024]{1,0:T(8,128)S(1)}, f32[256,1024]{1,0:T(8,128)}, u32[]{:S(2)}) copy-start(f32[256,1024]{1,0:T(8,128)} %copy-done.4) | copy-start | bytes 3145732
  (22 other events, 63.6 us)
Sparse Core Ops, SparseCore 0:
  11.0 59.3 all-gather.16
  73.2 55.3 all-gather.12
  131.5 55.3 all-gather.18
  188.9 44.7 all-gather.14
  235.1 44.6 all-gather.20
  282.7 55.1 all-gather.22
  340.7 66.1 all-gather.24
  409.7 66.2 all-gather.26
  478.9 66.2 all-gather.28
  547.2 44.8 all-gather.30
  593.7 45.5 all-gather.32
  642.0 146.6 reduce-scatter.13
  791.6 146.1 reduce-scatter.7
  940.5 146.5 reduce-scatter.9
  1089.8 145.9 reduce-scatter.11
  1238.6 249.8 reduce-scatter.15
  1491.2 248.4 reduce-scatter.17
  1742.4 248.4 reduce-scatter.19
where the time goes:
time: 2010 us; the launch traced here: 2000 us
  waiting for transfers between devices  1580 us (79%)
  matrix products  169 us (8%)
  blocking collectives  118 us (6%)
  local copies, waits for them, and re-layouts  73.6 us (4%)
  other arithmetic  32.3 us (2%)
    reduce_scatter x1, waiting for transfers between devices, per_device(): lax.psum_scatter(grad_gate, ('seq', 'ctx'), scatter_dimension=0, tiled=True)  253 us
    reduce_scatter x1, waiting for transfers between devices, per_device(): lax.psum_scatter(grad_down, ('seq', 'ctx'), scatter_dimension=0, tiled=True)  251 us
    reduce_scatter x1, waiting for transfers between devices, per_device(): lax.psum_scatter(grad_up, ('seq', 'ctx'), scatter_dimension=0, tiled=True)  251 us
    reduce_scatter x1, waiting for transfers between devices, per_device(): lax.psum_scatter(grad_key, ('seq', 'ctx'), scatter_dimension=0, tiled=True)  149 us
    reduce_scatter x1, waiting for transfers between devices, per_device(): lax.psum_scatter(grad_value, ('seq', 'ctx'), scatter_dimension=0, tiled=T...  149 us
    reduce_scatter x1, waiting for transfers between devices, per_device(): lax.psum_scatter(grad_query, ('seq', 'ctx'), scatter_dimension=0, tiled=T...  120 us
    unnamed x2, blocking collectives  81.1 us
    all_gather x1, waiting for transfers between devices, per_device(): lax.all_gather(own_weights[6], ('seq', 'ctx'), axis=0, tiled=True)  64.5 us
  transfers between devices with their start and end apart: 18, of which 16 were waited for; matrix products, arithmetic and copies ran while one was open for 13% of the time, Pallas kernels for 0%

commit v1 on v0

--- a/solution.py
+++ b/solution.py
@@ -1,6 +1,10 @@
+import types
+
 import jax
 import jax.numpy as jnp
 from jax import lax
+from jax.experimental import pallas as pl
+from jax.experimental.pallas import tpu as pltpu
 from jax.sharding import PartitionSpec as P
 
 HEADS = 16
@@ -320,9 +324,864 @@
     )
 
 
+BF = jnp.bfloat16
+F32 = jnp.float32
+MESH_ID = pl.DeviceIdType.MESH
+QC = 768
+GC = 1536
+BLK = 256
+
+
+def dot_nn(a, b):
+    return lax.dot_general(a, b, (((1,), (0,)), ((), ())), preferred_element_type=F32)
+
+
+def dot_nt(a, b):
+    return lax.dot_general(a, b, (((1,), (1,)), ((), ())), preferred_element_type=F32)
+
+
+def dot_tn(a, b):
+    return lax.dot_general(a, b, (((0,), (0,)), ((), ())), preferred_element_type=F32)
+
+
+N_SEM = 220
+VMEM_LIMIT = 64 * 2**20 - 2**18
+
+SCRATCH = dict(
+    TOK=((256, 1024), BF),
+    STT=((4, 8, 128), F32),
+    ST=((1024, 128), F32),
+    COS=((1024, 128), F32),
+    SIN=((1024, 128), F32),
+    FV=((1024, 256), BF),
+    COT=((1024, 1024), BF),
+    N1=((1024, 1024), BF),
+    N2=((1024, 1024), BF),
+    DB=((1024, 1024), BF),
+    GA=((2, 4, 4, 16, 128), BF),
+    GV=((8, 1024), F32),
+    WA=((2, 4, 4, 32, QC), BF),
+    WO=((2, 4, 32, 1024), BF),
+    WG=((2, 4, 4, 32, GC), BF),
+    WD=((2, 4, 96, 1024), BF),
+    QS=((1024, 256), BF),
+    KR=((1024, 256), BF),
+    V=((1024, 256), BF),
+    O=((1024, 256), BF),
+    DA=((1024, 256), BF),
+    P0=((4, 256, 256), BF),
+    P1=((4, 256, 512), BF),
+    P2=((4, 256, 768), BF),
+    P3=((4, 256, 1024), BF),
+    DQ=((1024, 256), BF),
+    DK=((1024, 256), F32),
+    DV=((1024, 256), F32),
+    DQKV=((1024, QC), BF),
+    H=((1024, 768), BF),
+    DGU=((1024, GC), BF),
+    RES=((256, 1024), F32),
+    DRES=((256, 1024), F32),
+    SSA=((2, 256, 1024), BF),
+    SRA=((2, 256, 1024), BF),
+    XSA=((256, 1024), BF),
+    XRA=((256, 1024), BF),
+    SSB=((2, 256, 1024), BF),
+    SRB=((2, 256, 1024), BF),
+    XSB=((256, 1024), BF),
+    XRB=((256, 1024), BF),
+    FF=((2, 256, 1024), F32),
+    OUT=((256, 1024), BF),
+    GQ=((4, 4, 32, QC), F32),
+    GO=((4, 32, 1024), F32),
+    GG=((4, 4, 32, GC), F32),
+    GD=((4, 96, 1024), F32),
+    RYQ=((4, 4, 32, QC), BF),
+    RYO=((4, 32, 1024), BF),
+    RYG=((4, 4, 32, GC), BF),
+    RYD=((4, 96, 1024), BF),
+    ZQ=((5, 4, 32, QC), BF),
+    ZO=((5, 32, 1024), BF),
+    ZG=((5, 4, 32, GC), BF),
+    ZD=((5, 96, 1024), BF),
+    GGS=((8, 1024), F32),
+    GGR=((3, 8, 1024), F32),
+    GGY=((8, 1024), F32),
+    GGT=((8, 1024), F32),
+    GGZ=((4, 8, 1024), F32),
+)
+
+
+def layer_kernel(*refs):
+    (tok, fv, cot, stt, gt, sa, sg, wo, wd) = refs[:9]
+    (o_block, o_gtok, o_gfv, o_gq, o_gg, o_go, o_gd, o_gain) = refs[9:17]
+    R = types.SimpleNamespace(**dict(zip(SCRATCH, refs[17:])))
+    ssem, rsem, lsem = refs[17 + len(SCRATCH) :]
+
+    s = lax.axis_index("seq")
+    z = lax.axis_index("ctx")
+    y = s // 4
+    j = s % 4
+    x = j // 2
+    k = j % 2
+    ny = 1 - y
+    sib = (4 * y + 2 * x + (1 - k), z)
+    xp = (4 * y + 2 * (1 - x) + k, z)
+    yp = (4 * ny + j, z)
+    home = (4 * y + z, 2 * k + (x + z) % 2)
+    away = (4 * y + 2 * ((z + j) % 2) + z // 2, j)
+    at_home = (home[0] == s) & (home[1] == z)
+    b_me = 2 * k + (x + z) % 2
+    b_x = 2 * k + (1 - x + z) % 2
+    b_s = 2 * (1 - k) + (x + z) % 2
+    b_xs = 2 * (1 - k) + (1 - x + z) % 2
+
+    counter = [0]
+    pend = []
+
+    def sems(n=1):
+        first = counter[0]
+        counter[0] += n
+        assert counter[0] <= N_SEM
+        return first
+
+    def rows(b):
+        return pl.ds(pl.multiple_of(b * BLK, BLK), BLK)
+
+    def rc(src, dst, i, dev, r=None):
+        return pltpu.make_async_remote_copy(
+            src_ref=src,
+            dst_ref=dst,
+            send_sem=ssem.at[i],
+            recv_sem=rsem.at[i if r is None else r],
+            device_id=dev,
+            device_id_type=MESH_ID,
+        )
+
+    def when(cond, fn):
+        if cond is None:
+            fn()
+        else:
+            pl.when(cond)(fn)
+
+    def start(desc, cond=None, keep=True):
+        when(cond, desc.start)
+        if keep:
+            pend.append((cond, desc))
+
+    barrier = pltpu.get_barrier_semaphore()
+    me = s * 4 + z
+
+    def greet(i, c):
+        t = (me + i) % 32
+        pl.semaphore_signal(barrier, inc=1, device_id=(t // 4, t % 4), device_id_type=MESH_ID)
+        return c
+
+    lax.fori_loop(1, 32, greet, 0)
+    pl.semaphore_wait(barrier, 31)
+
+    i_tok, i_cot, i_st, i_fv = sems(), sems(), sems(4), sems(8)
+
+    def route(src, dst, i, self_cond, dev, r=None):
+        when(self_cond, pltpu.make_async_copy(src, dst, rsem.at[i if r is None else r]).start)
+        start(rc(src, dst, i, dev, r), jnp.logical_not(self_cond))
+
+    def arrive(like_src, dst, i, self_cond, dev):
+        when(self_cond, pltpu.make_async_copy(like_src, dst, rsem.at[i]).wait)
+        when(jnp.logical_not(self_cond), rc(dst, dst, i, dev).wait_recv)
+
+    away_self = (away[0] == s) & (away[1] == z)
+    own_x = (z + j) % 2
+    b_away = z
+
+    def arrivals_tok():
+        arrive(tok, R.TOK, i_tok, at_home, home)
+
+    def group_dev(c, jj):
+        return (4 * y + c, jj)
+
+    route(tok, R.TOK, i_tok, away_self, away)
+    for c in range(4):
+        self_c = (j == z) & (j == c)
+        route(stt, R.STT.at[z], i_st + c, self_c, group_dev(c, j), i_st + z)
+
+    def spread(src, buf, base, dst_index):
+        for c in range(4):
+            start(rc(src.at[c], dst_index, base + c, group_dev(c, z), base + j), j != c)
+
+    i_gt, i_sa, i_sg = sems(4), sems(4), sems(4)
+    l_copies = []
+
+    def local(src, dst):
+        d = pltpu.make_async_copy(src, dst, lsem.at[len(l_copies)])
+        l_copies.append(d)
+        d.start()
+        return d
+
+    loc_gt = local(gt, R.GA.at[y, j, z])
+    for c in range(4):
+        start(rc(gt, R.GA.at[y, j, z], i_gt + c, group_dev(c, z), i_gt + j), j != c)
+    loc_sa = local(sa.at[j], R.WA.at[y, j, z])
+    spread(sa, R.WA, i_sa, R.WA.at[y, j, z])
+    loc_wo = local(wo, R.WO.at[y, z])
+    for c in range(4):
+        self_c = (j == z) & (j == c)
+        for h in range(2):
+            src = fv.at[:, pl.ds(128 * (c + 4 * h), 128)]
+            dst = R.FV.at[rows(z), pl.ds(128 * h, 128)]
+            route(src, dst, i_fv + 2 * c + h, self_c, group_dev(c, j), i_fv + 2 * z + h)
+    loc_sg = local(sg.at[j], R.WG.at[y, j, z])
+    spread(sg, R.WG, i_sg, R.WG.at[y, j, z])
+    loc_wd = local(wd, R.WD.at[y, z])
+    route(cot, R.COT.at[rows(b_away)], i_cot, away_self, away)
+
+    def wait_group(base, dst_of):
+        for c in range(4):
+            when(j != c, rc(dst_of(c), dst_of(c), base + c, sib).wait_recv)
+
+    class Gather:
+        def __init__(self, pieces):
+            self.pieces = pieces
+            n = len(pieces)
+            self.up, self.dn, self.ys = sems(4 * n), sems(4 * n), sems(4 * n)
+
+        def send(self, step):
+            zu, zd = z - step, z + step
+            cu, cd = zu >= 0, zd <= 3
+            for p, piece in enumerate(self.pieces):
+                if step < 3:
+                    src = piece(y, zu)
+                    start(
+                        rc(src, src, self.up + 4 * p + zu, (s, z + 1), self.up + 4 * p + zu),
+                        cu & (z < 3),
+                    )
+                    src = piece(y, zd)
+                    start(
+                        rc(src, src, self.dn + 4 * p + zd, (s, z - 1), self.dn + 4 * p + zd),
+                        cd & (z > 0),
+                    )
+                src = piece(y, zu)
+                start(rc(src, src, self.ys + 4 * p + zu, yp), cu)
+                if step > 0:
+                    src = piece(y, zd)
+                    start(rc(src, src, self.ys + 4 * p + zd, yp), cd)
+
+        def recv(self, step):
+            zu, zd = z - step, z + step
+            for p, piece in enumerate(self.pieces):
+                src = piece(y, zu)
+                when(zu >= 0, rc(src, src, self.up + 4 * p + zu, (s, z)).wait_recv)
+                src = piece(y, zd)
+                when(zd <= 3, rc(src, src, self.dn + 4 * p + zd, (s, z)).wait_recv)
+
+        def finish(self):
+            for p, piece in enumerate(self.pieces):
+                for zz in range(4):
+                    src = piece(ny, zz)
+                    rc(src, src, self.ys + 4 * p + zz, yp).wait_recv()
+
+    def cols(ref):
+        return lambda yy, zz: ref.at[yy, :, zz]
+
+    def rws(ref):
+        return lambda yy, zz: ref.at[yy, zz]
+
+    g_gain = Gather([cols(R.GA)])
+    g_attn = Gather([cols(R.WA), rws(R.WO)])
+    g_ffn = Gather([cols(R.WG), rws(R.WD)])
+
+    loc_gt.wait()
+    wait_group(i_gt, lambda c: R.GA.at[y, c, z])
+    g_gain.send(0)
+    loc_sa.wait()
+    loc_wo.wait()
+    wait_group(i_sa, lambda c: R.WA.at[y, c, z])
+    g_attn.send(0)
+    for step in (1, 2, 3):
+        g_gain.recv(step)
+        g_gain.send(step)
+        g_attn.recv(step)
+        g_attn.send(step)
+    loc_sg.wait()
+    loc_wd.wait()
+    wait_group(i_sg, lambda c: R.WG.at[y, c, z])
+    g_ffn.send(0)
+    g_gain.finish()
+    gains = jnp.zeros((16, 128), F32)
+    for yy in range(2):
+        for jj in range(4):
+            for zz in range(4):
+                gains = gains + R.GA[yy, jj, zz].astype(F32)
+    for r in range(8):
+        R.GV[0:1, 128 * r : 128 * r + 128] = gains[r : r + 1, :]
+        R.GV[1:2, 128 * r : 128 * r + 128] = gains[8 + r : 9 + r, :]
+
+    class Share:
+        def __init__(self, buf):
+            self.buf = buf
+            self.i = sems(3)
+
+        def piece(self, b):
+            return self.buf.at[rows(b)]
+
+        def send(self):
+            p = self.piece(b_me)
+            start(rc(p, p, self.i, xp))
+            start(rc(p, p, self.i + 1, sib))
+
+        def forward(self):
+            p = self.piece(b_x)
+            rc(p, p, self.i, xp).wait_recv()
+            start(rc(p, p, self.i + 2, sib))
+
+        def wait_sib(self):
+            p = self.piece(b_s)
+            rc(p, p, self.i + 1, sib).wait_recv()
+
+        def finish(self):
+            p = self.piece(b_xs)
+            rc(p, p, self.i + 2, sib).wait_recv()
+
+    arrivals_tok()
+    xs = R.TOK[...].astype(F32)
+    rs1 = lax.rsqrt(jnp.mean(xs * xs, axis=-1, keepdims=True) + norm_eps)
+    R.N1[rows(b_me), :] = (xs * rs1 * R.GV[0:1, :]).astype(BF)
+    sh1 = Share(R.N1)
+    sh1.send()
+    for c in range(4):
+        arrive(stt, R.STT.at[c], i_st + c, (j == z) & (c == z), home)
+    for b in range(4):
+        for r in range(2):
+            row = R.STT[b, r : r + 1, :]
+            R.ST[256 * b + 128 * r : 256 * b + 128 * r + 128, :] = jnp.transpose(
+                jnp.broadcast_to(row, (128, 128))
+            )
+    lane = lax.broadcasted_iota(jnp.int32, (1, 128), 1)
+    low_half = (lane % 64) < 32
+    freq = jnp.exp((lane % 32).astype(F32) * (-2.0 / HD * 9.210340371976184))
+
+    def angle_body(b, c):
+        pos = (lax.broadcasted_iota(jnp.int32, (BLK, 128), 0) + b * BLK).astype(F32)
+        ang = (pos - R.ST[rows(b), :]) * freq
+        R.COS[rows(b), :] = jnp.cos(ang)
+        R.SIN[rows(b), :] = jnp.where(low_half, -jnp.sin(ang), jnp.sin(ang))
+        return c
+
+    lax.fori_loop(0, 4, angle_body, 0)
+    sh1.forward()
+    g_ffn.recv(1)
+    g_ffn.send(1)
+
+    def turn(v):
+        return jnp.where(low_half, pltpu.roll(v, 96, 1), pltpu.roll(v, 32, 1))
+
+    for c in range(4):
+        self_c = (j == z) & (c == z)
+        for h in range(2):
+            src = fv.at[:, pl.ds(128 * (j + 4 * h), 128)]
+            dst = R.FV.at[rows(c), pl.ds(128 * h, 128)]
+            arrive(src, dst, i_fv + 2 * c + h, self_c, home)
+    g_attn.finish()
+    sh1.wait_sib()
+    sh1.finish()
+
+    def qkv_body(b, c):
+        raw = dot_nn(R.N1[rows(b), :], R.WA[...].reshape(1024, QC))
+        cs, sn = R.COS[rows(b), :], R.SIN[rows(b), :]
+        for t in range(2):
+            sl = slice(128 * t, 128 * t + 128)
+            q = raw[:, sl]
+            R.QS[rows(b), sl] = ((q * cs + turn(q) * sn).astype(BF).astype(F32) * 0.125).astype(
+                BF
+            )
+            kk = raw[:, 256 + 128 * t : 384 + 128 * t]
+            R.KR[rows(b), sl] = (kk * cs + turn(kk) * sn).astype(BF)
+        R.V[rows(b), :] = (
+            0.5 * raw[:, 512:768] + 0.5 * R.FV[rows(b), :].astype(F32)
+        ).astype(BF)
+        return c
+
+    lax.fori_loop(0, 4, qkv_body, 0)
+    g_ffn.recv(2)
+    g_ffn.send(2)
+
+    PB = [R.P0, R.P1, R.P2, R.P3]
+
+    def head_parts(h):
+        pair = pl.ds(pl.multiple_of((h // 2) * 128, 128), 128)
+        mine = ((lane // 64) == (h % 2)).astype(F32)
+        return pair, mine.astype(BF), mine
+
+    def attn_body(h, c):
+        pair, low_mine, mine = head_parts(h)
+        for i in range(4):
+            n = BLK * (i + 1)
+            q = R.QS[BLK * i : n, pair] * low_mine
+            sc = dot_nt(q, R.KR[0:n, pair])
+            col = lax.broadcasted_iota(jnp.int32, (BLK, n), 1)
+            row = lax.broadcasted_iota(jnp.int32, (BLK, n), 0) + BLK * i
+            first = R.ST[BLK * i : n, 0:1].astype(jnp.int32)
+            sc = jnp.where((col >= first) & (col <= row), sc, masked_score)
+            top = jnp.max(sc, axis=-1, keepdims=True)
+            e = jnp.exp(sc - top)
+            p = (e * (1.0 / jnp.sum(e, axis=-1, keepdims=True))).astype(BF)
+            PB[i][h] = p
+            o = dot_nn(p, R.V[0:n, pair]) * mine
+            R.O[BLK * i : n, pair] += o.astype(BF)
+        return c
+
+    R.O[...] = jnp.zeros((1024, 256), BF)
+    lax.fori_loop(0, 4, attn_body, 0)
+    g_ffn.recv(3)
+    g_ffn.send(3)
+
+    class GroupSum:
+        def __init__(self, bufs):
+            self.ss, self.sr, self.xs, self.xr = bufs
+            self.i = sems(3)
+
+        def run(self, fn):
+            ff = R.FF
+            self.ss[0] = fn(b_xs).astype(BF)
+            d0 = rc(self.ss.at[0], self.sr.at[0], self.i, sib)
+            d0.start()
+            self.ss[1] = fn(b_s).astype(BF)
+            d1 = rc(self.ss.at[1], self.sr.at[1], self.i + 1, sib)
+            d1.start()
+            ff[0] = fn(b_x)
+            d0.wait_recv()
+            self.xs[...] = (ff[0] + self.sr[0].astype(F32)).astype(BF)
+            d2 = rc(self.xs, self.xr, self.i + 2, xp)
+            d2.start()
+            ff[1] = fn(b_me)
+            d1.wait_recv()
+            ff[1] = ff[1] + self.sr[1].astype(F32)
+            self.descs = (d0, d1, d2)
+
+        def result(self):
+            d0, d1, d2 = self.descs
+            d2.wait_recv()
+            out = R.FF[1] + self.xr[...].astype(F32)
+            d0.wait_send()
+            d1.wait_send()
+            d2.wait_send()
+            return out
+
+    set_a = (R.SSA, R.SRA, R.XSA, R.XRA)
+    set_b = (R.SSB, R.SRB, R.XSB, R.XRB)
+    sum_attn = GroupSum(set_a)
+    sum_attn.run(lambda b: dot_nn(R.O[rows(b), :], R.WO[...].reshape(256, 1024)))
+    arrive(cot, R.COT.at[rows(b_me)], i_cot, at_home, home)
+    sh_cot = Share(R.COT)
+    sh_cot.send()
+    res = R.TOK[...].astype(F32) + sum_attn.result()
+    R.RES[...] = res
+    rs2 = lax.rsqrt(jnp.mean(res * res, axis=-1, keepdims=True) + norm_eps)
+    R.N2[rows(b_me), :] = (res * rs2 * R.GV[1:2, :]).astype(BF)
+    sh2 = Share(R.N2)
+    sh2.send()
+    sh_cot.forward()
+    sh_cot.wait_sib()
+    sh_cot.finish()
+    g_ffn.finish()
+    sh2.forward()
+    sh2.wait_sib()
+    sh2.finish()
+
+    def ffn_body(b, c):
+        gu = dot_nn(R.N2[rows(b), :], R.WG[...].reshape(1024, GC))
+        gate, up = gu[:, :768], gu[:, 768:]
+        sig = 1.0 / (1.0 + jnp.exp(-gate))
+        silu = gate * sig
+        R.H[rows(b), :] = (silu * up).astype(BF)
+        dh = dot_nt(R.COT[rows(b), :], R.WD[...].reshape(768, 1024))
+        R.DGU[rows(b), 0:768] = (dh * up * (sig * (1.0 + gate * (1.0 - sig)))).astype(BF)
+        R.DGU[rows(b), 768:1536] = (dh * silu).astype(BF)
+        return c
+
+    lax.fori_loop(0, 4, ffn_body, 0)
+    sum_dn2 = GroupSum(set_a)
+    sum_dn2.run(lambda b: dot_nt(R.DGU[rows(b), :], R.WG[...].reshape(1024, GC)))
+
+    class Reduce:
+        def __init__(self, g, ry, zr, is_cols):
+            self.g, self.ry, self.zr = g, ry, zr
+            self.is_cols = is_cols
+            self.iy, self.up, self.dn = sems(), sems(5), sems(5)
+
+        def send_y(self, sy):
+            self.sy = sy
+            start(rc(sy, self.ry, self.iy, yp))
+
+        def recv_y(self):
+            rc(self.ry, self.ry, self.iy, yp).wait_recv()
+
+        def term(self, o, c):
+            if self.is_cols:
+                return self.g[c, o] + self.ry[c, o].astype(F32)
+            return self.g[o] + self.ry[o].astype(F32)
+
+        def slot(self, o, c):
+            return self.zr.at[o, c] if self.is_cols else self.zr.at[o]
+
+        def chunks(self):
+            return range(4) if self.is_cols else range(1)
+
+        def hop(self, o, upward):
+            zr = self.zr
+            if upward:
+                cond, head, target = z < o, z == 0, (s, z + 1)
+                slot_in, slot_out, base = o, o, self.up
+            else:
+                cond, head, target = z > o, z == 3, (s, z - 1)
+                slot_in, base = o, self.dn
+                slot_out = jnp.where(z - 1 == o, 4, o)
+
+            def go():
+                @pl.when(jnp.logical_not(head))
+                def _():
+                    rc(zr.at[slot_in], zr.at[slot_in], base + slot_in, (s, z)).wait_recv()
+                    for c in self.chunks():
+                        self.slot(o, c)[...] = (
+                            self.term(o, c) + self.slot(o, c)[...].astype(F32)
+                        ).astype(BF)
+
+                @pl.when(head)
+                def _():
+                    for c in self.chunks():
+                        self.slot(o, c)[...] = self.term(o, c).astype(BF)
+
+                rc(zr.at[o], zr.at[slot_out], base + o, target, base + slot_out).start()
+
+            pl.when(cond)(go)
+            pend.append((cond, rc(zr.at[o], zr.at[slot_out], base + o, target, base + slot_out)))
+
+        def last(self, put):
+            zr = self.zr
+
+            @pl.when(z > 0)
+            def _():
+                rc(zr.at[z], zr.at[z], self.up + z, (s, z)).wait_recv()
+
+            @pl.when(z == 0)
+            def _():
+                for c in self.chunks():
+                    self.slot(z, c)[...] = jnp.zeros(self.slot(z, c).shape, BF)
+
+            @pl.when(z < 3)
+            def _():
+                rc(zr.at[4], zr.at[4], self.dn + 4, (s, z)).wait_recv()
+
+            @pl.when(z == 3)
+            def _():
+                for c in self.chunks():
+                    self.slot(4, c)[...] = jnp.zeros(self.slot(4, c).shape, BF)
+
+            for c in self.chunks():
+                put(
+                    c,
+                    self.term(z, c)
+                    + self.slot(z, c)[...].astype(F32)
+                    + self.slot(4, c)[...].astype(F32),
+                )
+
+        def chain(self, put):
+            for o_up, o_dn in ((3, 0), (2, 1), (1, 2)):
+                self.hop(o_up, True)
+                self.hop(o_dn, False)
+            self.last(put)
+
+    def half(yy, width):
+        return pl.ds(pl.multiple_of(yy * width, width), width)
+
+    def grad_cols(left, right, red, sy):
+        width = right.shape[1]
+        for yy, keep in ((ny, False), (y, True)):
+            for m in range(2):
+                a = left[:, pl.ds(pl.multiple_of(yy * 512 + 256 * m, 256), 256)]
+                val = dot_tn(a, right[...]).reshape(2, 4, 32, width)
+                if keep:
+                    red.g[2 * m : 2 * m + 2] = val
+                else:
+                    sy[2 * m : 2 * m + 2] = val.astype(BF)
+            if not keep:
+                red.send_y(sy)
+
+    def grad_rows(left, right, red, sy, per):
+        for yy, keep in ((ny, False), (y, True)):
+            a = left[:, half(yy, 4 * per)]
+            val = dot_tn(a, right[...]).reshape(4, per, 1024)
+            if keep:
+                red.g[...] = val
+            else:
+                sy[...] = val.astype(BF)
+                red.send_y(sy)
+
+    red_g = Reduce(R.GG, R.RYG, R.ZG, True)
+    red_d = Reduce(R.GD, R.RYD, R.ZD, False)
+    red_o = Reduce(R.GO, R.RYO, R.ZO, False)
+    red_q = Reduce(R.GQ, R.RYQ, R.ZQ, True)
+
+    dn2 = sum_dn2.result()
+    res = R.RES[...]
+    rs2 = lax.rsqrt(jnp.mean(res * res, axis=-1, keepdims=True) + norm_eps)
+    xh = res * rs2
+    gd = dn2 * R.GV[1:2, :]
+    R.GGS[...] = jnp.zeros((8, 1024), F32)
+    R.GGS[1:2, :] = jnp.sum(dn2 * xh, axis=0, keepdims=True)
+    dres = (
+        R.COT[rows(b_me), :].astype(F32)
+        + rs2 * (gd - xh * jnp.mean(gd * xh, axis=-1, keepdims=True))
+    )
+    R.DRES[...] = dres
+    R.DB[rows(b_me), :] = dres.astype(BF)
+    sh3 = Share(R.DB)
+    sh3.send()
+    for cond, desc in pend:
+        when(cond, desc.wait_send)
+    pend.clear()
+    sum_out = GroupSum(set_b)
+    sum_out.run(lambda b: dot_nn(R.H[rows(b), :], R.WD[...].reshape(768, 1024)))
+    R.OUT[...] = (R.RES[...] + sum_out.result()).astype(BF)
+    i_out = sems()
+    route(R.OUT, o_block, i_out, at_home, home)
+    grad_rows(R.H, R.COT, red_d, R.WD.at[0], 96)
+    grad_cols(R.N2, R.DGU, red_g, R.WG.at[0])
+    sh3.forward()
+    sh3.wait_sib()
+    sh3.finish()
+
+    def da_body(b, c):
+        R.DA[rows(b), :] = dot_nt(R.DB[rows(b), :], R.WO[...].reshape(256, 1024)).astype(
+            BF
+        )
+        return c
+
+    lax.fori_loop(0, 4, da_body, 0)
+    grad_rows(R.O, R.DB, red_o, R.WO.at[0], 32)
+    red_d.recv_y()
+    red_g.recv_y()
+
+    def put_rows(ref):
+        def put(c, val):
+            ref[...] = val
+
+        return put
+
+    red_d.chain(put_rows(R.GD.at[0]))
+    R.DK[...] = jnp.zeros((1024, 256), F32)
+    R.DV[...] = jnp.zeros((1024, 256), F32)
+
+    def back_body(h, c):
+        pair, low_mine, mine = head_parts(h)
+        for i in range(4):
+            n = BLK * (i + 1)
+            do = R.DA[BLK * i : n, pair] * low_mine
+            q = R.QS[BLK * i : n, pair] * low_mine
+            dp = dot_nt(do, R.V[0:n, pair])
+            pb = PB[i][h]
+            p = pb.astype(F32)
+            delta = jnp.sum(p * dp, axis=-1, keepdims=True)
+            ds = (p * (dp - delta)).astype(BF)
+            dq = dot_nn(ds, R.KR[0:n, pair]) * (0.125 * mine)
+            R.DQ[BLK * i : n, pair] += dq.astype(BF)
+            R.DK[0:n, pair] += dot_tn(ds, q)
+            R.DV[0:n, pair] += dot_tn(pb, do)
+        return c
+
+    R.DQ[...] = jnp.zeros((1024, 256), BF)
+    lax.fori_loop(0, 4, back_body, 0)
+
+    def dqkv_body(b, c):
+        cs, sn = R.COS[rows(b), :], R.SIN[rows(b), :]
+        for t in range(2):
+            sl = slice(128 * t, 128 * t + 128)
+            u = R.DQ[rows(b), sl].astype(F32)
+            R.DQKV[rows(b), sl] = (u * cs - turn(u) * sn).astype(BF)
+            u = R.DK[rows(b), sl].astype(BF).astype(F32)
+            R.DQKV[rows(b), 256 + 128 * t : 384 + 128 * t] = (u * cs - turn(u) * sn).astype(BF)
+        R.DQKV[rows(b), 512:768] = (
+            0.5 * R.DV[rows(b), :].astype(BF).astype(F32)
+        ).astype(BF)
+        return c
+
+    lax.fori_loop(0, 4, dqkv_body, 0)
+    i_gf = sems(8)
+    for b in range(4):
+        self_b = (j == z) & (z == b)
+        for h in range(2):
+            src = R.DQKV.at[pl.ds(256 * b, 256), pl.ds(512 + 128 * h, 128)]
+            dst = o_gfv.at[:, pl.ds(pl.multiple_of(128 * (j + 4 * h), 128), 128)]
+            route(src, dst, i_gf + 2 * b + h, self_b, (4 * y + z, b), i_gf + 2 * j + h)
+    sum_dn1 = GroupSum(set_a)
+    sum_dn1.run(lambda b: dot_nt(R.DQKV[rows(b), :], R.WA[...].reshape(1024, QC)))
+    grad_cols(R.N1, R.DQKV, red_q, R.WA.at[0])
+
+    dn1 = sum_dn1.result()
+    xs = R.TOK[...].astype(F32)
+    rs1 = lax.rsqrt(jnp.mean(xs * xs, axis=-1, keepdims=True) + norm_eps)
+    xh = xs * rs1
+    gd = dn1 * R.GV[0:1, :]
+    R.GGS[0:1, :] = jnp.sum(dn1 * xh, axis=0, keepdims=True)
+    R.XSB[...] = (
+        R.DRES[...] + rs1 * (gd - xh * jnp.mean(gd * xh, axis=-1, keepdims=True))
+    ).astype(BF)
+    i_gtok = sems()
+    route(R.XSB, o_gtok, i_gtok, at_home, home)
+
+    i_ggg, i_ggy, i_ggz = sems(4), sems(), sems(4)
+    for c in range(4):
+        start(
+            rc(R.GGS, R.GGR.at[(j - c - 1) % 4], i_ggg + c, group_dev(c, z), i_ggg + j),
+            j != c,
+        )
+    def put_cols(ref):
+        def put(c, val):
+            ref[c, 0] = val
+
+        return put
+
+    red_g.chain(put_cols(R.GG))
+    red_o.recv_y()
+    red_q.recv_y()
+    for c in range(4):
+        slot = R.GGR.at[(c - j - 1) % 4]
+        when(j != c, rc(slot, slot, i_ggg + c, sib).wait_recv)
+    R.GGT[...] = R.GGS[...] + R.GGR[0] + R.GGR[1] + R.GGR[2]
+    start(rc(R.GGT, R.GGY, i_ggy, yp))
+    red_o.chain(put_rows(R.GO.at[0]))
+    rc(R.GGY, R.GGY, i_ggy, yp).wait_recv()
+    R.GGZ[z] = R.GGT[...] + R.GGY[...]
+    for c in range(4):
+        start(rc(R.GGZ.at[z], R.GGZ.at[z], i_ggz + c, (s, c), i_ggz + z), z != c)
+    red_q.chain(put_cols(R.GQ))
+
+    i_rg, i_rq = sems(4), sems(4)
+    outs = []
+
+    def hand_back(g, send, out, base):
+        for c in range(4):
+            send[c] = g[c, 0].astype(BF)
+        for c in range(4):
+            start(rc(send.at[c], out.at[j], base + c, group_dev(c, z), base + j), j != c)
+        d = pltpu.make_async_copy(send.at[j], out.at[j], lsem.at[10 + len(outs)])
+        d.start()
+        outs.append(d)
+
+    hand_back(R.GG, R.RYG.at[0], o_gg, i_rg)
+    hand_back(R.GQ, R.RYQ.at[0], o_gq, i_rq)
+    for ref, out in ((R.GO, o_go), (R.GD, o_gd)):
+        d = pltpu.make_async_copy(ref.at[0], out, lsem.at[10 + len(outs)])
+        d.start()
+        outs.append(d)
+    for c in range(4):
+        when(z != c, rc(R.GGZ.at[c], R.GGZ.at[c], i_ggz + c, (s, z)).wait_recv)
+    R.GGY[...] = R.GGZ[0] + R.GGZ[1] + R.GGZ[2] + R.GGZ[3]
+    d = pltpu.make_async_copy(R.GGY, o_gain, lsem.at[10 + len(outs)])
+    d.start()
+    outs.append(d)
+
+    arrive(R.OUT, o_block, i_out, away_self, away)
+    arrive(R.XSB, o_gtok, i_gtok, away_self, away)
+    for c in range(4):
+        self_c = (j == z) & (j == c)
+        for h in range(2):
+            src = R.DQKV.at[pl.ds(256 * z, 256), pl.ds(512 + 128 * h, 128)]
+            dst = o_gfv.at[:, pl.ds(pl.multiple_of(128 * (c + 4 * h), 128), 128)]
+            arrive(src, dst, i_gf + 2 * c + h, self_c, home)
+    wait_group(i_rg, lambda c: o_gg.at[c])
+    wait_group(i_rq, lambda c: o_gq.at[c])
+    for d in outs:
+        d.wait()
+    for cond, desc in pend:
+        when(cond, desc.wait_send)
+
+
+def slot_map():
+    r = lax.broadcasted_iota(jnp.int32, (1408, 1536), 0)
+    c = lax.broadcasted_iota(jnp.int32, (1408, 1536), 1)
+    return ((r // 88 == c // 96) & (r % 88 == c % 96)).astype(BF)
+
+
+def fast_device(
+    tokens,
+    first_values,
+    gain_attn,
+    w_query,
+    w_key,
+    w_value,
+    w_out,
+    gain_ffn,
+    w_gate,
+    w_up,
+    w_down,
+    segment_start,
+    cotangent,
+):
+    d = lax.axis_index("seq") * 4 + lax.axis_index("ctx")
+    place = slot_map()
+    sa = jnp.stack([w_query, w_key, w_value]).reshape(3, 32, 2, 4, 128)
+    sa = sa.transpose(3, 1, 0, 2, 4).reshape(4, 32, QC)
+    gu = jnp.stack([w_gate, w_up]).reshape(128, 1408)
+    gu = dot_nn(gu, place).astype(BF).reshape(2, 32, 2, 4, 384)
+    sg = gu.transpose(3, 1, 0, 2, 4).reshape(4, 32, GC)
+    wd = jnp.pad(w_down, ((0, 8), (0, 0)))
+
+    def spot(g):
+        return lax.dynamic_update_slice(jnp.zeros((1024,), BF), g, (32 * d,)).reshape(8, 128)
+
+    gt = jnp.concatenate([spot(gain_attn), spot(gain_ffn)])
+    stt = jnp.pad(segment_start.astype(F32).reshape(2, 128), ((0, 6), (0, 0)))
+    hbm = pl.BlockSpec(memory_space=pl.ANY)
+    outs = pl.pallas_call(
+        layer_kernel,
+        name="layer",
+        out_shape=[
+            jax.ShapeDtypeStruct((256, 1024), BF),
+            jax.ShapeDtypeStruct((256, 1024), BF),
+            jax.ShapeDtypeStruct((256, 1024), BF),
+            jax.ShapeDtypeStruct((4, 32, QC), BF),
+            jax.ShapeDtypeStruct((4, 32, GC), BF),
+            jax.ShapeDtypeStruct((32, 1024), F32),
+            jax.ShapeDtypeStruct((96, 1024), F32),
+            jax.ShapeDtypeStruct((8, 1024), F32),
+        ],
+        in_specs=[hbm] * 9,
+        out_specs=[hbm] * 8,
+        scratch_shapes=[pltpu.VMEM(shape, dtype) for shape, dtype in SCRATCH.values()]
+        + [
+            pltpu.SemaphoreType.DMA((N_SEM,)),
+            pltpu.SemaphoreType.DMA((N_SEM,)),
+            pltpu.SemaphoreType.DMA((20,)),
+        ],
+        compiler_params=pltpu.CompilerParams(
+            collective_id=0, has_side_effects=True, vmem_limit_bytes=VMEM_LIMIT
+        ),
+    )(tokens, first_values, cotangent, stt, gt, sa, sg, w_out, wd)
+    block_out, grad_tokens, grad_first, gq, gg, grad_out, gd, gains = outs
+    gq = gq.reshape(4, 32, 3, 2, 128).transpose(2, 1, 3, 0, 4).reshape(3, 32, 1024).astype(F32)
+    gg = gg.reshape(4, 32, 2, 2, 384).transpose(2, 1, 3, 0, 4).reshape(128, 1536)
+    gg = dot_nt(gg, place).reshape(2, 32, 2816)
+    own_gains = lax.dynamic_slice(gains, (0, 32 * d), (2, 32))
+    return (
+        block_out,
+        grad_tokens,
+        grad_first,
+        own_gains[0],
+        gq[0],
+        gq[1],
+        gq[2],
+        grad_out,
+        own_gains[1],
+        gg[0],
+        gg[1],
+        gd[:88],
+    )
+
+
 def solution(mesh):
+    fits = mesh.shape["seq"] == 8 and mesh.shape["ctx"] == 4
     return jax.shard_map(
-        per_device,
+        fast_device if fits else per_device,
         mesh=mesh,
         in_specs=(
             P(("seq", "ctx"), None),

time: 2010 us -> 463 us (0.23)
  waiting for transfers between devices: 1580 us -> 0 us
  Pallas kernels: 0 us -> 427 us
  matrix products: 169 us -> 3 us
  blocking collectives: 118 us -> 0 us
  local copies, waits for them, and re-layouts: 73.6 us -> 17 us
  other arithmetic: 32.3 us -> 5.91 us
    reduce_scatter x7 -> x0, waiting for transfers between devices: 1170 us -> none  [the longest x1 253 us: per_device(): lax.psum_scatter(grad_gate, ('seq', 'ctx'), scatter_dimension=0, tiled=True)]
    pallas_call x0 -> x1, Pallas kernels: none -> 427 us  [fast_device(): pl.pallas_call(layer_kernel, name='layer', out_shape=[jax.ShapeDtypeStruc...]
    all_gather x11 -> x0, waiting for transfers between devices: 399 us -> none  [the longest x1 64.5 us: per_device(): lax.all_gather(own_weights[6], ('seq', 'ctx'), axis=0, tiled=True)]
    dot_general x35 -> x2, matrix products: 169 us -> 3 us  [the longest x1 1.56 us: dot_nt(): lax.dot_general(a, b, (((1,), (1,)), ((), ())), preferred_element_type=F32)]
    unnamed x2 -> x0, blocking collectives: 81.1 us -> none
    all_gather x3 -> x0, blocking collectives: 36.7 us -> none  [the longest x1 13.6 us: per_device(): lax.all_gather(log_total.T.astype(jnp.bfloat16), 'ctx', axis=0, tiled=True)]
    unnamed x79 -> x35, local copies, waits for them, and re-layouts: 30 us -> 3.16 us
    reshape x4 -> x7, local copies, waits for them, and re-layouts: 25.5 us -> 3.88 us  [the longest x2 1.6 us: fast_device(): gg.reshape(4, 32, 2, 2, 384).transpose(2, 1, 3, 0, 4).reshape(128, 1536)]
  transfers between devices with their start and end apart: 18 -> 0, of which waited for: 16 -> 0; matrix products, arithmetic and copies ran while one was open for 13% -> 0% of each run, Pallas kernels for 0% -> 0%
where the time goes in v1:
time: 463 us; the launch traced here: 454 us
  Pallas kernels  427 us (92%)
  local copies, waits for them, and re-layouts  17 us (4%)
  other arithmetic  5.91 us (1%)
    pallas_call x1, Pallas kernels, fast_device(): pl.pallas_call(layer_kernel, name='layer', out_shape=[jax.ShapeDtypeStruc...  427 us

profile of v1, /device:TPU:0, one launch (start us, length us, event | category | flops | bytes accessed | tf_op | source)
XLA Modules:
  0.0 454.3 jit_solution(659568357016170576)
XLA Ops:
  0.7 1.0 dynamic_update_slice.6
  1.6 0.8 dynamic_update_slice.7
  2.5 0.6 pad_maximum_fusion.1.refs_4_
  3.1 4.9 %fusion = pred[1408,1536]{1,0:T(32,128)(4,1)S(1)} fusion(s32[1536]{0:T(1024)S(1)} %get-tuple-element.36, s32[1536]{0:T(1024)S(1)} %get-tuple-element.41, s32[1408]{0:T(1024)S(1)} %get-tuple-element.38, s32[1408]{0:T(1024)S(1)} %get-tuple-element.39, s32[1536]{0:T(1024)S(1)} %get-tuple-element.35, s32[1536]{0:T(1024)S(1)} %get-tuple-element.42, ...), kind=kLoop, calls=%fused_computation.2 | loop fusion | flops 15138816 | bytes 2215680 | tf_op jit(solution)/shard_map/and | solution.py:1102
  8.1 0.1 reshape.78
  8.3 1.4 convolution_convert_fusion
  9.8 0.1 reshape.79
  9.9 0.3 copy.42
  10.2 1.0 reshape.80.refs_6_
  11.5 0.3 maximum_bitcast_fusion
  11.8 0.8 reshape.77.refs_5_
  12.6 0.7 pad.9.refs_8_
  13.3 0.6 pad.8.refs_3_
  13.9 426.9 %layer.1 = (bf16[256,1024]{1,0:T(8,128)(2,1)}, bf16[256,1024]{1,0:T(8,128)(2,1)}, bf16[256,1024]{1,0:T(8,128)(2,1)}, bf16[4,32,768]{2,1,0:T(8,128)(2,1)}, bf16[4...) custom-call(bf16[256,1024]{1,0:T(8,128)(2,1)} %refs_0_.1, ...), custom_call_target="tpu_custom_call" | custom-call | tf_op jit(solution)/shard_map/layer/pallas_call | solution.py:1135
  440.8 0.9 constant_dynamic-slice_fusion
  441.8 0.5 slice_bitcast_fusion
  442.3 1.1 reshape.81
  443.4 0.5 copy.39
  444.0 1.6 fusion.15
  445.6 0.8 squeeze.26
  446.4 0.8 squeeze.27
  447.3 0.2 reshape.83
  447.5 0.1 fusion.14
  447.6 0.1 copy.36
  447.7 0.7 squeeze.22
  448.5 0.7 squeeze.23
  449.3 0.7 squeeze.24
  450.0 0.8 slice.36
  450.8 0.8 copy.53
  451.6 0.8 copy.54
  452.4 0.8 copy.55
  453.2 0.7 copy.56
  (50 shorter events, 0.7 us)
Async XLA Ops:
  0.6 7.4 %copy-start.9 = (bf16[32,2816]{1,0:T(8,128)(2,1)S(1)}, bf16[32,2816]{1,0:T(8,128)(2,1)}, u32[]{:S(2)}) copy-start(bf16[32,2816]{1,0:T(8,128)(2,1)} %param.21) | copy-start | bytes 540676
  0.7 7.4 %copy-start.8 = (bf16[32,2816]{1,0:T(8,128)(2,1)S(1)}, bf16[32,2816]{1,0:T(8,128)(2,1)}, u32[]{:S(2)}) copy-start(bf16[32,2816]{1,0:T(8,128)(2,1)} %param.22) | copy-start | bytes 540676
  8.1 1.7 copy-start
  8.3 2.9 copy-start.11
  9.7 1.6 copy-start.12
  9.8 1.7 copy-start.13
  9.8 2.8 copy-start.7
  9.8 3.5 copy-start.14
  440.8 3.1 copy-start.1
  445.5 1.8 copy-start.6
  445.6 4.5 copy-start.5
  446.4 4.4 copy-start.4
  447.5 4.1 copy-start.3
  447.6 4.8 %copy-start.2 = (bf16[256,1024]{1,0:T(8,128)(2,1)S(1)}, bf16[256,1024]{1,0:T(8,128)(2,1)}, u32[]{:S(2)}) copy-start(bf16[256,1024]{1,0:T(8,128)(2,1)} %get-tuple-element.61) | copy-start | bytes 1572868
  449.2 4.0 copy-start.10

commit v2 on v1

--- a/solution.py
+++ b/solution.py
@@ -344,7 +344,17 @@
     return lax.dot_general(a, b, (((0,), (0,)), ((), ())), preferred_element_type=F32)
 
 
-N_SEM = 220
+N_SEM = 360
+LAG = 6.5
+T_D = 2.0
+T_1 = 8.0
+T_2 = 18.0
+T_3 = 22.0
+T_4 = 30.0
+T_5 = 48.0
+T_6 = 56.0
+T_7 = 62.0
+T_8 = 76.0
 VMEM_LIMIT = 64 * 2**20 - 2**18
 
 SCRATCH = dict(
@@ -358,7 +368,10 @@
     N1=((1024, 1024), BF),
     N2=((1024, 1024), BF),
     DB=((1024, 1024), BF),
-    GA=((2, 4, 4, 16, 128), BF),
+    GAZ=((4, 16, 128), BF),
+    GAS=((2, 16, 128), BF),
+    GAJ=((4, 16, 128), BF),
+    SYD=((4, 96, 1024), BF),
     GV=((8, 1024), F32),
     WA=((2, 4, 4, 32, QC), BF),
     WO=((2, 4, 32, 1024), BF),
@@ -427,25 +440,38 @@
     sib = (4 * y + 2 * x + (1 - k), z)
     xp = (4 * y + 2 * (1 - x) + k, z)
     yp = (4 * ny + j, z)
+    up_z, dn_z = (s, z + 1), (s, z - 1)
+    column = (z + k) % 2
+    crossing = x != column
+    direct = x == column
+    jp = 2 * (1 - x) + k
+
+    def host(jj):
+        return (4 * y + 2 * column + z // 2, jj)
+
     home = (4 * y + z, 2 * k + (x + z) % 2)
-    away = (4 * y + 2 * ((z + j) % 2) + z // 2, j)
     at_home = (home[0] == s) & (home[1] == z)
+    away = host(j)
+    away_self = (away[0] == s) & (away[1] == z)
     b_me = 2 * k + (x + z) % 2
     b_x = 2 * k + (1 - x + z) % 2
     b_s = 2 * (1 - k) + (x + z) % 2
     b_xs = 2 * (1 - k) + (1 - x + z) % 2
 
-    counter = [0]
+    counters = [0, 0]
     pend = []
 
     def sems(n=1):
-        first = counter[0]
-        counter[0] += n
-        assert counter[0] <= N_SEM
+        first = counters[0]
+        counters[0] += n
+        assert counters[0] <= N_SEM
         return first
 
     def rows(b):
         return pl.ds(pl.multiple_of(b * BLK, BLK), BLK)
+
+    def half_rows(b, h):
+        return pl.ds(pl.multiple_of(b * BLK + 128 * h, 128), 128)
 
     def rc(src, dst, i, dev, r=None):
         return pltpu.make_async_remote_copy(
@@ -463,10 +489,29 @@
         else:
             pl.when(cond)(fn)
 
-    def start(desc, cond=None, keep=True):
+    def start(desc, cond=None):
         when(cond, desc.start)
-        if keep:
-            pend.append((cond, desc))
+        pend.append((cond, desc))
+
+    def local(src, dst):
+        d = pltpu.make_async_copy(src, dst, lsem.at[counters[1]])
+        counters[1] += 1
+        d.start()
+        return d
+
+    def both(p, q):
+        return q if p is None else p & q
+
+    def route(src, dst, i, self_cond, dev, r, cond=None):
+        when(both(cond, self_cond), pltpu.make_async_copy(src, dst, rsem.at[r]).start)
+        start(rc(src, dst, i, dev, r), both(cond, jnp.logical_not(self_cond)))
+
+    def arrive(like_src, dst, r, self_cond):
+        when(self_cond, pltpu.make_async_copy(like_src, dst, rsem.at[r]).wait)
+        when(jnp.logical_not(self_cond), rc(dst, dst, r, sib).wait_recv)
+
+    def group_dev(c, jj):
+        return (4 * y + c, jj)
 
     barrier = pltpu.get_barrier_semaphore()
     me = s * 4 + z
@@ -479,141 +524,188 @@
     lax.fori_loop(1, 32, greet, 0)
     pl.semaphore_wait(barrier, 31)
 
-    i_tok, i_cot, i_st, i_fv = sems(), sems(), sems(4), sems(8)
-
-    def route(src, dst, i, self_cond, dev, r=None):
-        when(self_cond, pltpu.make_async_copy(src, dst, rsem.at[i if r is None else r]).start)
-        start(rc(src, dst, i, dev, r), jnp.logical_not(self_cond))
-
-    def arrive(like_src, dst, i, self_cond, dev):
-        when(self_cond, pltpu.make_async_copy(like_src, dst, rsem.at[i]).wait)
-        when(jnp.logical_not(self_cond), rc(dst, dst, i, dev).wait_recv)
-
-    away_self = (away[0] == s) & (away[1] == z)
-    own_x = (z + j) % 2
-    b_away = z
-
-    def arrivals_tok():
-        arrive(tok, R.TOK, i_tok, at_home, home)
-
-    def group_dev(c, jj):
-        return (4 * y + c, jj)
-
-    route(tok, R.TOK, i_tok, away_self, away)
+    i_gz, i_gy, i_gj = sems(4), sems(), sems(4)
+    loc_gt = local(gt, R.GAZ.at[z])
+    for c in range(4):
+        start(rc(gt, R.GAZ.at[z], i_gz + c, (s, c), i_gz + z), z != c)
+
+    class Move:
+        def __init__(self, src, stage, pieces, arrivals):
+            self.src, self.stage, self.pieces, self.arrivals = src, stage, pieces, arrivals
+            self.ix = sems(2)
+            self.io, self.ir = sems(8), sems(8)
+
+        def cross(self):
+            for h in range(2):
+                cut = pl.ds(128 * h, 128)
+                start(rc(self.src.at[cut], self.stage.at[cut], self.ix + h, xp), crossing)
+
+        def own(self):
+            for n, (cut, dst, self_cond, dev, r) in enumerate(self.pieces(j)):
+                route(self.src.at[cut], dst, self.io + n, self_cond, dev, r, direct)
+
+        def relay(self):
+            def take():
+                for h in range(2):
+                    part = self.stage.at[pl.ds(128 * h, 128)]
+                    rc(part, part, self.ix + h, xp).wait_recv()
+
+            pl.when(direct)(take)
+            for n, (cut, dst, self_cond, dev, r) in enumerate(self.pieces(jp)):
+                route(self.stage.at[cut], dst, self.ir + n, self_cond, dev, r, direct)
+
+        def wait(self):
+            for like, dst, r, self_cond in self.arrivals():
+                arrive(like, dst, r, self_cond)
+
+    last_hop_self = (z % 2 == k) & (b_me == z)
+
+    def block_pieces(dst_at, base):
+        def pieces(jj):
+            dev = host(jj)
+            self_cond = (dev[0] == s) & (dev[1] == z)
+            return [
+                (pl.ds(128 * h, 128), dst_at(z, h), self_cond, dev, base + h) for h in range(2)
+            ]
+
+        return pieces
+
+    def block_arrivals(src, dst_at, base):
+        return lambda: [
+            (src.at[pl.ds(128 * h, 128)], dst_at(b_me, h), base + h, last_hop_self)
+            for h in range(2)
+        ]
+
+    def tok_at(b, h):
+        return R.TOK.at[pl.ds(128 * h, 128)]
+
+    def cot_at(b, h):
+        return R.COT.at[half_rows(b, h)]
+
+    def fv_at(b, h):
+        return R.FV.at[rows(b), pl.ds(128 * h, 128)]
+
+    i_tok, i_cot, i_fv, i_st = sems(2), sems(2), sems(8), sems(4)
+
+    def fv_pieces(jj):
+        out = []
+        for c in range(4):
+            dev = group_dev(c, jj)
+            self_cond = (dev[0] == s) & (dev[1] == z)
+            for h in range(2):
+                cut = (slice(None), pl.ds(128 * (c + 4 * h), 128))
+                out.append((cut, fv_at(z, h), self_cond, dev, i_fv + 2 * z + h))
+        return out
+
+    def fv_arrivals():
+        out = []
+        for b in range(4):
+            self_cond = (z % 2 == k) & (z == b) & (x == (b + k) % 2)
+            for h in range(2):
+                out.append((fv.at[:, pl.ds(128 * h, 128)], fv_at(b, h), i_fv + 2 * b + h, self_cond))
+        return out
+
+    m_tok = Move(tok, R.DB.at[0:256], block_pieces(tok_at, i_tok), block_arrivals(tok, tok_at, i_tok))
+    m_cot = Move(cot, R.DB.at[512:768], block_pieces(cot_at, i_cot), block_arrivals(cot, cot_at, i_cot))
+    m_fv = Move(fv, R.DB.at[256:512], fv_pieces, fv_arrivals)
+
+    m_tok.cross()
+    m_tok.own()
     for c in range(4):
         self_c = (j == z) & (j == c)
         route(stt, R.STT.at[z], i_st + c, self_c, group_dev(c, j), i_st + z)
 
-    def spread(src, buf, base, dst_index):
-        for c in range(4):
-            start(rc(src.at[c], dst_index, base + c, group_dev(c, z), base + j), j != c)
-
-    i_gt, i_sa, i_sg = sems(4), sems(4), sems(4)
-    l_copies = []
-
-    def local(src, dst):
-        d = pltpu.make_async_copy(src, dst, lsem.at[len(l_copies)])
-        l_copies.append(d)
-        d.start()
-        return d
-
-    loc_gt = local(gt, R.GA.at[y, j, z])
-    for c in range(4):
-        start(rc(gt, R.GA.at[y, j, z], i_gt + c, group_dev(c, z), i_gt + j), j != c)
+    i_sa, i_sg = sems(4), sems(4)
     loc_sa = local(sa.at[j], R.WA.at[y, j, z])
-    spread(sa, R.WA, i_sa, R.WA.at[y, j, z])
     loc_wo = local(wo, R.WO.at[y, z])
     for c in range(4):
-        self_c = (j == z) & (j == c)
-        for h in range(2):
-            src = fv.at[:, pl.ds(128 * (c + 4 * h), 128)]
-            dst = R.FV.at[rows(z), pl.ds(128 * h, 128)]
-            route(src, dst, i_fv + 2 * c + h, self_c, group_dev(c, j), i_fv + 2 * z + h)
+        start(rc(sa.at[c], R.WA.at[y, j, z], i_sa + c, group_dev(c, z), i_sa + j), j != c)
+    loc_wd = local(wd, R.WD.at[y, z])
     loc_sg = local(sg.at[j], R.WG.at[y, j, z])
-    spread(sg, R.WG, i_sg, R.WG.at[y, j, z])
-    loc_wd = local(wd, R.WD.at[y, z])
-    route(cot, R.COT.at[rows(b_away)], i_cot, away_self, away)
+    for c in range(4):
+        start(rc(sg.at[c], R.WG.at[y, j, z], i_sg + c, group_dev(c, z), i_sg + j), j != c)
+    m_fv.cross()
 
     def wait_group(base, dst_of):
         for c in range(4):
             when(j != c, rc(dst_of(c), dst_of(c), base + c, sib).wait_recv)
 
     class Gather:
-        def __init__(self, pieces):
-            self.pieces = pieces
-            n = len(pieces)
-            self.up, self.dn, self.ys = sems(4 * n), sems(4 * n), sems(4 * n)
-
-        def send(self, step):
+        def __init__(self, piece):
+            self.piece = piece
+            self.up, self.dn, self.ys = sems(4), sems(4), sems(4)
+
+        def send_z(self, step):
             zu, zd = z - step, z + step
-            cu, cd = zu >= 0, zd <= 3
-            for p, piece in enumerate(self.pieces):
-                if step < 3:
-                    src = piece(y, zu)
-                    start(
-                        rc(src, src, self.up + 4 * p + zu, (s, z + 1), self.up + 4 * p + zu),
-                        cu & (z < 3),
-                    )
-                    src = piece(y, zd)
-                    start(
-                        rc(src, src, self.dn + 4 * p + zd, (s, z - 1), self.dn + 4 * p + zd),
-                        cd & (z > 0),
-                    )
-                src = piece(y, zu)
-                start(rc(src, src, self.ys + 4 * p + zu, yp), cu)
-                if step > 0:
-                    src = piece(y, zd)
-                    start(rc(src, src, self.ys + 4 * p + zd, yp), cd)
+            src = self.piece(y, zu)
+            start(rc(src, src, self.up + zu, up_z), (zu >= 0) & (z < 3))
+            src = self.piece(y, zd)
+            start(rc(src, src, self.dn + zd, dn_z), (zd <= 3) & (z > 0))
+
+        def send_y(self, step):
+            zu, zd = z - step, z + step
+            src = self.piece(y, zu)
+            start(rc(src, src, self.ys + zu, yp), zu >= 0)
+            if step > 0:
+                src = self.piece(y, zd)
+                start(rc(src, src, self.ys + zd, yp), zd <= 3)
 
         def recv(self, step):
             zu, zd = z - step, z + step
-            for p, piece in enumerate(self.pieces):
-                src = piece(y, zu)
-                when(zu >= 0, rc(src, src, self.up + 4 * p + zu, (s, z)).wait_recv)
-                src = piece(y, zd)
-                when(zd <= 3, rc(src, src, self.dn + 4 * p + zd, (s, z)).wait_recv)
+            src = self.piece(y, zu)
+            when(zu >= 0, rc(src, src, self.up + zu, sib).wait_recv)
+            src = self.piece(y, zd)
+            when(zd <= 3, rc(src, src, self.dn + zd, sib).wait_recv)
+
+        def pass_on(self, step):
+            self.recv(step)
+            if step < 3:
+                self.send_z(step)
+            self.send_y(step)
 
         def finish(self):
-            for p, piece in enumerate(self.pieces):
-                for zz in range(4):
-                    src = piece(ny, zz)
-                    rc(src, src, self.ys + 4 * p + zz, yp).wait_recv()
-
-    def cols(ref):
-        return lambda yy, zz: ref.at[yy, :, zz]
-
-    def rws(ref):
-        return lambda yy, zz: ref.at[yy, zz]
-
-    g_gain = Gather([cols(R.GA)])
-    g_attn = Gather([cols(R.WA), rws(R.WO)])
-    g_ffn = Gather([cols(R.WG), rws(R.WD)])
+            for zz in range(4):
+                src = self.piece(ny, zz)
+                rc(src, src, self.ys + zz, yp).wait_recv()
+
+    g_a = Gather(lambda yy, zz: R.WA.at[yy, :, zz])
+    g_o = Gather(lambda yy, zz: R.WO.at[yy, zz])
+    g_d = Gather(lambda yy, zz: R.WD.at[yy, zz])
+    g_g0 = Gather(lambda yy, zz: R.WG.at[yy, 0:2, zz])
+    g_g1 = Gather(lambda yy, zz: R.WG.at[yy, 2:4, zz])
 
     loc_gt.wait()
-    wait_group(i_gt, lambda c: R.GA.at[y, c, z])
-    g_gain.send(0)
+    for c in range(4):
+        slot = R.GAZ.at[c]
+        when(z != c, rc(slot, slot, i_gz + c, sib).wait_recv)
+    R.GAS[0] = R.GAZ[0] + R.GAZ[1] + R.GAZ[2] + R.GAZ[3]
+    start(rc(R.GAS.at[0], R.GAS.at[1], i_gy, yp))
+
+    wait_group(i_sa, lambda c: R.WA.at[y, c, z])
     loc_sa.wait()
     loc_wo.wait()
-    wait_group(i_sa, lambda c: R.WA.at[y, c, z])
-    g_attn.send(0)
-    for step in (1, 2, 3):
-        g_gain.recv(step)
-        g_gain.send(step)
-        g_attn.recv(step)
-        g_attn.send(step)
-    loc_sg.wait()
+    g_a.send_z(0)
+    g_a.send_y(0)
+    g_o.send_z(0)
+    g_o.send_y(0)
+
+    rc(R.GAS.at[1], R.GAS.at[1], i_gy, yp).wait_recv()
+    R.GAJ[j] = R.GAS[0] + R.GAS[1]
+    for c in range(4):
+        start(rc(R.GAJ.at[j], R.GAJ.at[j], i_gj + c, group_dev(c, z), i_gj + j), j != c)
+    m_tok.relay()
     loc_wd.wait()
-    wait_group(i_sg, lambda c: R.WG.at[y, c, z])
-    g_ffn.send(0)
-    g_gain.finish()
-    gains = jnp.zeros((16, 128), F32)
-    for yy in range(2):
-        for jj in range(4):
-            for zz in range(4):
-                gains = gains + R.GA[yy, jj, zz].astype(F32)
+    g_d.send_y(0)
+    wait_group(i_gj, lambda c: R.GAJ.at[c])
+    gains = (R.GAJ[0] + R.GAJ[1] + R.GAJ[2] + R.GAJ[3]).astype(F32)
     for r in range(8):
         R.GV[0:1, 128 * r : 128 * r + 128] = gains[r : r + 1, :]
         R.GV[1:2, 128 * r : 128 * r + 128] = gains[8 + r : 9 + r, :]
+    wait_group(i_sg, lambda c: R.WG.at[y, c, z])
+    loc_sg.wait()
+    g_a.pass_on(1)
+    g_o.pass_on(1)
+    g_g0.send_y(0)
 
     class Share:
         def __init__(self, buf):
@@ -641,14 +733,22 @@
             p = self.piece(b_xs)
             rc(p, p, self.i + 2, sib).wait_recv()
 
-    arrivals_tok()
+    m_tok.wait()
     xs = R.TOK[...].astype(F32)
     rs1 = lax.rsqrt(jnp.mean(xs * xs, axis=-1, keepdims=True) + norm_eps)
     R.N1[rows(b_me), :] = (xs * rs1 * R.GV[0:1, :]).astype(BF)
     sh1 = Share(R.N1)
     sh1.send()
+    m_cot.cross()
+    g_a.pass_on(2)
+    g_o.pass_on(2)
+    g_g1.send_y(0)
+    m_fv.own()
+    m_fv.relay()
+    for g in (g_d, g_g0, g_g1):
+        g.send_z(0)
     for c in range(4):
-        arrive(stt, R.STT.at[c], i_st + c, (j == z) & (c == z), home)
+        arrive(stt, R.STT.at[c], i_st + c, (j == z) & (c == z))
     for b in range(4):
         for r in range(2):
             row = R.STT[b, r : r + 1, :]
@@ -667,22 +767,17 @@
         return c
 
     lax.fori_loop(0, 4, angle_body, 0)
+    g_a.pass_on(3)
+    g_o.pass_on(3)
     sh1.forward()
-    g_ffn.recv(1)
-    g_ffn.send(1)
 
     def turn(v):
         return jnp.where(low_half, pltpu.roll(v, 96, 1), pltpu.roll(v, 32, 1))
 
-    for c in range(4):
-        self_c = (j == z) & (c == z)
-        for h in range(2):
-            src = fv.at[:, pl.ds(128 * (j + 4 * h), 128)]
-            dst = R.FV.at[rows(c), pl.ds(128 * h, 128)]
-            arrive(src, dst, i_fv + 2 * c + h, self_c, home)
-    g_attn.finish()
+    g_a.finish()
     sh1.wait_sib()
     sh1.finish()
+    m_fv.wait()
 
     def qkv_body(b, c):
         raw = dot_nn(R.N1[rows(b), :], R.WA[...].reshape(1024, QC))
@@ -690,19 +785,17 @@
         for t in range(2):
             sl = slice(128 * t, 128 * t + 128)
             q = raw[:, sl]
-            R.QS[rows(b), sl] = ((q * cs + turn(q) * sn).astype(BF).astype(F32) * 0.125).astype(
-                BF
-            )
+            R.QS[rows(b), sl] = ((q * cs + turn(q) * sn).astype(BF).astype(F32) * 0.125).astype(BF)
             kk = raw[:, 256 + 128 * t : 384 + 128 * t]
             R.KR[rows(b), sl] = (kk * cs + turn(kk) * sn).astype(BF)
-        R.V[rows(b), :] = (
-            0.5 * raw[:, 512:768] + 0.5 * R.FV[rows(b), :].astype(F32)
-        ).astype(BF)
+        R.V[rows(b), :] = (0.5 * raw[:, 512:768] + 0.5 * R.FV[rows(b), :].astype(F32)).astype(BF)
         return c
 
     lax.fori_loop(0, 4, qkv_body, 0)
-    g_ffn.recv(2)
-    g_ffn.send(2)
+    for g in (g_d, g_g0, g_g1):
+        g.pass_on(1)
+    m_cot.own()
+    m_cot.relay()
 
     PB = [R.P0, R.P1, R.P2, R.P3]
 
@@ -730,9 +823,10 @@
         return c
 
     R.O[...] = jnp.zeros((1024, 256), BF)
-    lax.fori_loop(0, 4, attn_body, 0)
-    g_ffn.recv(3)
-    g_ffn.send(3)
+    lax.fori_loop(0, 2, attn_body, 0)
+    for g in (g_d, g_g0, g_g1):
+        g.pass_on(2)
+    lax.fori_loop(2, 4, attn_body, 0)
 
     class GroupSum:
         def __init__(self, bufs):
@@ -744,14 +838,14 @@
             self.ss[0] = fn(b_xs).astype(BF)
             d0 = rc(self.ss.at[0], self.sr.at[0], self.i, sib)
             d0.start()
-            self.ss[1] = fn(b_s).astype(BF)
-            d1 = rc(self.ss.at[1], self.sr.at[1], self.i + 1, sib)
-            d1.start()
             ff[0] = fn(b_x)
             d0.wait_recv()
             self.xs[...] = (ff[0] + self.sr[0].astype(F32)).astype(BF)
             d2 = rc(self.xs, self.xr, self.i + 2, xp)
             d2.start()
+            self.ss[1] = fn(b_s).astype(BF)
+            d1 = rc(self.ss.at[1], self.sr.at[1], self.i + 1, sib)
+            d1.start()
             ff[1] = fn(b_me)
             d1.wait_recv()
             ff[1] = ff[1] + self.sr[1].astype(F32)
@@ -768,24 +862,28 @@
 
     set_a = (R.SSA, R.SRA, R.XSA, R.XRA)
     set_b = (R.SSB, R.SRB, R.XSB, R.XRB)
+    g_o.finish()
     sum_attn = GroupSum(set_a)
     sum_attn.run(lambda b: dot_nn(R.O[rows(b), :], R.WO[...].reshape(256, 1024)))
-    arrive(cot, R.COT.at[rows(b_me)], i_cot, at_home, home)
+    m_cot.wait()
     sh_cot = Share(R.COT)
-    sh_cot.send()
+    g_d.pass_on(3)
     res = R.TOK[...].astype(F32) + sum_attn.result()
     R.RES[...] = res
     rs2 = lax.rsqrt(jnp.mean(res * res, axis=-1, keepdims=True) + norm_eps)
     R.N2[rows(b_me), :] = (res * rs2 * R.GV[1:2, :]).astype(BF)
     sh2 = Share(R.N2)
     sh2.send()
+    sh_cot.send()
+    g_g0.pass_on(3)
+    g_g1.pass_on(3)
+    sh2.forward()
     sh_cot.forward()
-    sh_cot.wait_sib()
-    sh_cot.finish()
-    g_ffn.finish()
-    sh2.forward()
-    sh2.wait_sib()
-    sh2.finish()
+    for g in (g_d, g_g0, g_g1):
+        g.finish()
+    for sh in (sh2, sh_cot):
+        sh.wait_sib()
+        sh.finish()
 
     def ffn_body(b, c):
         gu = dot_nn(R.N2[rows(b), :], R.WG[...].reshape(1024, GC))
@@ -799,127 +897,157 @@
         return c
 
     lax.fori_loop(0, 4, ffn_body, 0)
+    for cond, desc in pend:
+        when(cond, desc.wait_send)
+    pend.clear()
+
+    events = []
+
+    class Reduce:
+        def __init__(self, g, sy, ry, zr, cs):
+            self.g, self.sy, self.ry, self.zr = g, sy, ry, zr
+            self.cs = cs
+            self.iy, self.up, self.dn = sems(4), sems(5), sems(5)
+
+        def cut(self, ref, o):
+            if self.cs is None:
+                return ref.at[o]
+            return ref.at[self.cs[0] : self.cs[1], o]
+
+        def zslot(self, o):
+            if self.cs is None:
+                return self.zr.at[o]
+            return self.zr.at[o, self.cs[0] : self.cs[1]]
+
+        def chunks(self):
+            return [None] if self.cs is None else range(*self.cs)
+
+        def chunk(self, o, c):
+            return self.zr.at[o] if c is None else self.zr.at[o, c]
+
+        def term(self, o, c):
+            at = o if c is None else (c, o)
+            return self.g[at] + self.ry[at].astype(F32)
+
+        def send_y(self):
+            for o in (3, 0, 2, 1):
+                start(rc(self.cut(self.sy, o), self.cut(self.ry, o), self.iy + o, yp))
+
+        def recv_y(self, o):
+            p = self.cut(self.ry, o)
+            rc(p, p, self.iy + o, yp).wait_recv()
+
+        def hop(self, o, upward, zz):
+            if upward:
+                head, target, base, slot_out = zz == 0, up_z, self.up, o
+            else:
+                head, target, base = zz == 3, dn_z, self.dn
+                slot_out = 4 if zz - 1 == o else o
+            d = rc(self.zslot(o), self.zslot(slot_out), base + o, target, base + slot_out)
+
+            def go():
+                if not head:
+                    p = self.zslot(o)
+                    rc(p, p, base + o, sib).wait_recv()
+                for c in self.chunks():
+                    p = self.chunk(o, c)
+                    val = self.term(o, c)
+                    if not head:
+                        val = val + p[...].astype(F32)
+                    p[...] = val.astype(BF)
+                d.start()
+
+            pl.when(z == zz)(go)
+            pend.append((z == zz, d))
+
+        def last(self, zz, put):
+            def go():
+                if zz > 0:
+                    p = self.zslot(zz)
+                    rc(p, p, self.up + zz, sib).wait_recv()
+                if zz < 3:
+                    p = self.zslot(4)
+                    rc(p, p, self.dn + 4, sib).wait_recv()
+                for c in self.chunks():
+                    val = self.term(zz, c)
+                    if zz > 0:
+                        val = val + self.chunk(zz, c)[...].astype(F32)
+                    if zz < 3:
+                        val = val + self.chunk(4, c)[...].astype(F32)
+                    put(c, val)
+
+            pl.when(z == zz)(go)
+
+        def schedule(self, t0, dt, lag, put):
+            for n, o in enumerate((3, 0, 2, 1)):
+                t = t0 + (n + 1) * dt
+                events.append((t, lambda o=o: self.recv_y(o)))
+                for zz in range(o):
+                    events.append((t + 0.01 + zz * lag, lambda o=o, zz=zz: self.hop(o, True, zz)))
+                for zz in range(3, o, -1):
+                    events.append(
+                        (t + 0.02 + (3 - zz) * lag, lambda o=o, zz=zz: self.hop(o, False, zz))
+                    )
+                events.append(
+                    (t + 0.03 + max(o, 3 - o) * lag, lambda o=o: self.last(o, put))
+                )
+
+    def run_until(t):
+        events.sort(key=lambda e: e[0])
+        while events and events[0][0] <= t:
+            events.pop(0)[1]()
+
+    def half(yy, width):
+        return pl.ds(pl.multiple_of(yy * width, width), width)
+
+    def grad_cols(left, right, g, sy, yy, m, keep):
+        width = right.shape[1]
+        a = left[:, pl.ds(pl.multiple_of(yy * 512 + 256 * m, 256), 256)]
+        val = dot_tn(a, right[...]).reshape(2, 4, 32, width)
+        if keep:
+            g[2 * m : 2 * m + 2] = val
+        else:
+            sy[2 * m : 2 * m + 2] = val.astype(BF)
+
+    def grad_rows(left, right, g, sy, yy, per, keep):
+        a = left[:, half(yy, 4 * per)]
+        val = dot_tn(a, right[...]).reshape(4, per, 1024)
+        if keep:
+            g[...] = val
+        else:
+            sy[...] = val.astype(BF)
+
+    red_d = Reduce(R.GD, R.SYD, R.RYD, R.ZD, None)
+    red_g0 = Reduce(R.GG, R.WG.at[0], R.RYG, R.ZG, (0, 2))
+    red_g1 = Reduce(R.GG, R.WG.at[0], R.RYG, R.ZG, (2, 4))
+    red_o = Reduce(R.GO, R.WO.at[0], R.RYO, R.ZO, None)
+    red_q = Reduce(R.GQ, R.WA.at[0], R.RYQ, R.ZQ, (0, 4))
+
+    def put_rows(ref):
+        def put(c, val):
+            ref[...] = val
+
+        return put
+
+    def put_cols(ref):
+        def put(c, val):
+            ref[c, 0] = val
+
+        return put
+
     sum_dn2 = GroupSum(set_a)
     sum_dn2.run(lambda b: dot_nt(R.DGU[rows(b), :], R.WG[...].reshape(1024, GC)))
-
-    class Reduce:
-        def __init__(self, g, ry, zr, is_cols):
-            self.g, self.ry, self.zr = g, ry, zr
-            self.is_cols = is_cols
-            self.iy, self.up, self.dn = sems(), sems(5), sems(5)
-
-        def send_y(self, sy):
-            self.sy = sy
-            start(rc(sy, self.ry, self.iy, yp))
-
-        def recv_y(self):
-            rc(self.ry, self.ry, self.iy, yp).wait_recv()
-
-        def term(self, o, c):
-            if self.is_cols:
-                return self.g[c, o] + self.ry[c, o].astype(F32)
-            return self.g[o] + self.ry[o].astype(F32)
-
-        def slot(self, o, c):
-            return self.zr.at[o, c] if self.is_cols else self.zr.at[o]
-
-        def chunks(self):
-            return range(4) if self.is_cols else range(1)
-
-        def hop(self, o, upward):
-            zr = self.zr
-            if upward:
-                cond, head, target = z < o, z == 0, (s, z + 1)
-                slot_in, slot_out, base = o, o, self.up
-            else:
-                cond, head, target = z > o, z == 3, (s, z - 1)
-                slot_in, base = o, self.dn
-                slot_out = jnp.where(z - 1 == o, 4, o)
-
-            def go():
-                @pl.when(jnp.logical_not(head))
-                def _():
-                    rc(zr.at[slot_in], zr.at[slot_in], base + slot_in, (s, z)).wait_recv()
-                    for c in self.chunks():
-                        self.slot(o, c)[...] = (
-                            self.term(o, c) + self.slot(o, c)[...].astype(F32)
-                        ).astype(BF)
-
-                @pl.when(head)
-                def _():
-                    for c in self.chunks():
-                        self.slot(o, c)[...] = self.term(o, c).astype(BF)
-
-                rc(zr.at[o], zr.at[slot_out], base + o, target, base + slot_out).start()
-
-            pl.when(cond)(go)
-            pend.append((cond, rc(zr.at[o], zr.at[slot_out], base + o, target, base + slot_out)))
-
-        def last(self, put):
-            zr = self.zr
-
-            @pl.when(z > 0)
-            def _():
-                rc(zr.at[z], zr.at[z], self.up + z, (s, z)).wait_recv()
-
-            @pl.when(z == 0)
-            def _():
-                for c in self.chunks():
-                    self.slot(z, c)[...] = jnp.zeros(self.slot(z, c).shape, BF)
-
-            @pl.when(z < 3)
-            def _():
-                rc(zr.at[4], zr.at[4], self.dn + 4, (s, z)).wait_recv()
-
-            @pl.when(z == 3)
-            def _():
-                for c in self.chunks():
-                    self.slot(4, c)[...] = jnp.zeros(self.slot(4, c).shape, BF)
-
-            for c in self.chunks():
-                put(
-                    c,
-                    self.term(z, c)
-                    + self.slot(z, c)[...].astype(F32)
-                    + self.slot(4, c)[...].astype(F32),
-                )
-
-        def chain(self, put):
-            for o_up, o_dn in ((3, 0), (2, 1), (1, 2)):
-                self.hop(o_up, True)
-                self.hop(o_dn, False)
-            self.last(put)
-
-    def half(yy, width):
-        return pl.ds(pl.multiple_of(yy * width, width), width)
-
-    def grad_cols(left, right, red, sy):
-        width = right.shape[1]
-        for yy, keep in ((ny, False), (y, True)):
-            for m in range(2):
-                a = left[:, pl.ds(pl.multiple_of(yy * 512 + 256 * m, 256), 256)]
-                val = dot_tn(a, right[...]).reshape(2, 4, 32, width)
-                if keep:
-                    red.g[2 * m : 2 * m + 2] = val
-                else:
-                    sy[2 * m : 2 * m + 2] = val.astype(BF)
-            if not keep:
-                red.send_y(sy)
-
-    def grad_rows(left, right, red, sy, per):
-        for yy, keep in ((ny, False), (y, True)):
-            a = left[:, half(yy, 4 * per)]
-            val = dot_tn(a, right[...]).reshape(4, per, 1024)
-            if keep:
-                red.g[...] = val
-            else:
-                sy[...] = val.astype(BF)
-                red.send_y(sy)
-
-    red_g = Reduce(R.GG, R.RYG, R.ZG, True)
-    red_d = Reduce(R.GD, R.RYD, R.ZD, False)
-    red_o = Reduce(R.GO, R.RYO, R.ZO, False)
-    red_q = Reduce(R.GQ, R.RYQ, R.ZQ, True)
+    grad_rows(R.H, R.COT, None, R.SYD, ny, 96, False)
+    red_d.send_y()
+    for m, red in ((0, red_g0), (1, red_g1)):
+        grad_cols(R.N2, R.DGU, None, R.WG.at[0], ny, m, False)
+        red.send_y()
+    grad_rows(R.H, R.COT, R.GD, None, y, 96, True)
+    for m in range(2):
+        grad_cols(R.N2, R.DGU, R.GG, None, y, m, True)
+    red_d.schedule(T_D, 4.3, LAG, put_rows(R.GD.at[0]))
+    red_g0.schedule(T_D + 4 * 4.3, 4.3, LAG, put_cols(R.GG))
+    red_g1.schedule(T_D + 8 * 4.3, 4.3, LAG, put_cols(R.GG))
 
     dn2 = sum_dn2.result()
     res = R.RES[...]
@@ -928,46 +1056,34 @@
     gd = dn2 * R.GV[1:2, :]
     R.GGS[...] = jnp.zeros((8, 1024), F32)
     R.GGS[1:2, :] = jnp.sum(dn2 * xh, axis=0, keepdims=True)
-    dres = (
-        R.COT[rows(b_me), :].astype(F32)
-        + rs2 * (gd - xh * jnp.mean(gd * xh, axis=-1, keepdims=True))
+    dres = R.COT[rows(b_me), :].astype(F32) + rs2 * (
+        gd - xh * jnp.mean(gd * xh, axis=-1, keepdims=True)
     )
     R.DRES[...] = dres
     R.DB[rows(b_me), :] = dres.astype(BF)
     sh3 = Share(R.DB)
     sh3.send()
-    for cond, desc in pend:
-        when(cond, desc.wait_send)
-    pend.clear()
+    run_until(T_1)
     sum_out = GroupSum(set_b)
     sum_out.run(lambda b: dot_nn(R.H[rows(b), :], R.WD[...].reshape(768, 1024)))
-    R.OUT[...] = (R.RES[...] + sum_out.result()).astype(BF)
-    i_out = sems()
-    route(R.OUT, o_block, i_out, at_home, home)
-    grad_rows(R.H, R.COT, red_d, R.WD.at[0], 96)
-    grad_cols(R.N2, R.DGU, red_g, R.WG.at[0])
+    run_until(T_2)
     sh3.forward()
     sh3.wait_sib()
     sh3.finish()
 
     def da_body(b, c):
-        R.DA[rows(b), :] = dot_nt(R.DB[rows(b), :], R.WO[...].reshape(256, 1024)).astype(
-            BF
-        )
+        R.DA[rows(b), :] = dot_nt(R.DB[rows(b), :], R.WO[...].reshape(256, 1024)).astype(BF)
         return c
 
     lax.fori_loop(0, 4, da_body, 0)
-    grad_rows(R.O, R.DB, red_o, R.WO.at[0], 32)
-    red_d.recv_y()
-    red_g.recv_y()
-
-    def put_rows(ref):
-        def put(c, val):
-            ref[...] = val
-
-        return put
-
-    red_d.chain(put_rows(R.GD.at[0]))
+    grad_rows(R.O, R.DB, None, R.WO.at[0], ny, 32, False)
+    red_o.send_y()
+    grad_rows(R.O, R.DB, R.GO, None, y, 32, True)
+    red_o.schedule(T_D + 12 * 4.3, 1.4, LAG, put_rows(R.GO.at[0]))
+    run_until(T_3)
+    R.OUT[...] = (R.RES[...] + sum_out.result()).astype(BF)
+    i_out = sems()
+    route(R.OUT, o_block, i_out, at_home, home, i_out)
     R.DK[...] = jnp.zeros((1024, 256), F32)
     R.DV[...] = jnp.zeros((1024, 256), F32)
 
@@ -989,7 +1105,9 @@
         return c
 
     R.DQ[...] = jnp.zeros((1024, 256), BF)
-    lax.fori_loop(0, 4, back_body, 0)
+    lax.fori_loop(0, 2, back_body, 0)
+    run_until(T_4)
+    lax.fori_loop(2, 4, back_body, 0)
 
     def dqkv_body(b, c):
         cs, sn = R.COS[rows(b), :], R.SIN[rows(b), :]
@@ -999,12 +1117,18 @@
             R.DQKV[rows(b), sl] = (u * cs - turn(u) * sn).astype(BF)
             u = R.DK[rows(b), sl].astype(BF).astype(F32)
             R.DQKV[rows(b), 256 + 128 * t : 384 + 128 * t] = (u * cs - turn(u) * sn).astype(BF)
-        R.DQKV[rows(b), 512:768] = (
-            0.5 * R.DV[rows(b), :].astype(BF).astype(F32)
-        ).astype(BF)
+        R.DQKV[rows(b), 512:768] = (0.5 * R.DV[rows(b), :].astype(BF).astype(F32)).astype(BF)
         return c
 
     lax.fori_loop(0, 4, dqkv_body, 0)
+    sum_dn1 = GroupSum(set_a)
+    sum_dn1.run(lambda b: dot_nt(R.DQKV[rows(b), :], R.WA[...].reshape(1024, QC)))
+    for m in range(2):
+        grad_cols(R.N1, R.DQKV, None, R.WA.at[0], ny, m, False)
+    red_q.send_y()
+    for m in range(2):
+        grad_cols(R.N1, R.DQKV, R.GQ, None, y, m, True)
+    red_q.schedule(T_D + 12 * 4.3 + 8, 4.3, LAG, put_cols(R.GQ))
     i_gf = sems(8)
     for b in range(4):
         self_b = (j == z) & (z == b)
@@ -1012,9 +1136,7 @@
             src = R.DQKV.at[pl.ds(256 * b, 256), pl.ds(512 + 128 * h, 128)]
             dst = o_gfv.at[:, pl.ds(pl.multiple_of(128 * (j + 4 * h), 128), 128)]
             route(src, dst, i_gf + 2 * b + h, self_b, (4 * y + z, b), i_gf + 2 * j + h)
-    sum_dn1 = GroupSum(set_a)
-    sum_dn1.run(lambda b: dot_nt(R.DQKV[rows(b), :], R.WA[...].reshape(1024, QC)))
-    grad_cols(R.N1, R.DQKV, red_q, R.WA.at[0])
+    run_until(T_5)
 
     dn1 = sum_dn1.result()
     xs = R.TOK[...].astype(F32)
@@ -1026,34 +1148,24 @@
         R.DRES[...] + rs1 * (gd - xh * jnp.mean(gd * xh, axis=-1, keepdims=True))
     ).astype(BF)
     i_gtok = sems()
-    route(R.XSB, o_gtok, i_gtok, at_home, home)
+    route(R.XSB, o_gtok, i_gtok, at_home, home, i_gtok)
 
     i_ggg, i_ggy, i_ggz = sems(4), sems(), sems(4)
     for c in range(4):
         start(
-            rc(R.GGS, R.GGR.at[(j - c - 1) % 4], i_ggg + c, group_dev(c, z), i_ggg + j),
-            j != c,
+            rc(R.GGS, R.GGR.at[(j - c - 1) % 4], i_ggg + c, group_dev(c, z), i_ggg + j), j != c
         )
-    def put_cols(ref):
-        def put(c, val):
-            ref[c, 0] = val
-
-        return put
-
-    red_g.chain(put_cols(R.GG))
-    red_o.recv_y()
-    red_q.recv_y()
+    run_until(T_6)
     for c in range(4):
         slot = R.GGR.at[(c - j - 1) % 4]
         when(j != c, rc(slot, slot, i_ggg + c, sib).wait_recv)
     R.GGT[...] = R.GGS[...] + R.GGR[0] + R.GGR[1] + R.GGR[2]
     start(rc(R.GGT, R.GGY, i_ggy, yp))
-    red_o.chain(put_rows(R.GO.at[0]))
+    run_until(T_7)
     rc(R.GGY, R.GGY, i_ggy, yp).wait_recv()
     R.GGZ[z] = R.GGT[...] + R.GGY[...]
     for c in range(4):
         start(rc(R.GGZ.at[z], R.GGZ.at[z], i_ggz + c, (s, c), i_ggz + z), z != c)
-    red_q.chain(put_cols(R.GQ))
 
     i_rg, i_rq = sems(4), sems(4)
     outs = []
@@ -1061,33 +1173,28 @@
     def hand_back(g, send, out, base):
         for c in range(4):
             send[c] = g[c, 0].astype(BF)
-        for c in range(4):
             start(rc(send.at[c], out.at[j], base + c, group_dev(c, z), base + j), j != c)
-        d = pltpu.make_async_copy(send.at[j], out.at[j], lsem.at[10 + len(outs)])
-        d.start()
-        outs.append(d)
-
+        outs.append(local(send.at[j], out.at[j]))
+
+    run_until(T_8)
     hand_back(R.GG, R.RYG.at[0], o_gg, i_rg)
+    outs.append(local(R.GD.at[0], o_gd))
+    run_until(1e9)
     hand_back(R.GQ, R.RYQ.at[0], o_gq, i_rq)
-    for ref, out in ((R.GO, o_go), (R.GD, o_gd)):
-        d = pltpu.make_async_copy(ref.at[0], out, lsem.at[10 + len(outs)])
-        d.start()
-        outs.append(d)
+    outs.append(local(R.GO.at[0], o_go))
     for c in range(4):
-        when(z != c, rc(R.GGZ.at[c], R.GGZ.at[c], i_ggz + c, (s, z)).wait_recv)
+        when(z != c, rc(R.GGZ.at[c], R.GGZ.at[c], i_ggz + c, sib).wait_recv)
     R.GGY[...] = R.GGZ[0] + R.GGZ[1] + R.GGZ[2] + R.GGZ[3]
-    d = pltpu.make_async_copy(R.GGY, o_gain, lsem.at[10 + len(outs)])
-    d.start()
-    outs.append(d)
-
-    arrive(R.OUT, o_block, i_out, away_self, away)
-    arrive(R.XSB, o_gtok, i_gtok, away_self, away)
+    outs.append(local(R.GGY, o_gain))
+
+    arrive(R.OUT, o_block, i_out, away_self)
+    arrive(R.XSB, o_gtok, i_gtok, away_self)
     for c in range(4):
         self_c = (j == z) & (j == c)
         for h in range(2):
             src = R.DQKV.at[pl.ds(256 * z, 256), pl.ds(512 + 128 * h, 128)]
             dst = o_gfv.at[:, pl.ds(pl.multiple_of(128 * (c + 4 * h), 128), 128)]
-            arrive(src, dst, i_gf + 2 * c + h, self_c, home)
+            arrive(src, dst, i_gf + 2 * c + h, self_c)
     wait_group(i_rg, lambda c: o_gg.at[c])
     wait_group(i_rq, lambda c: o_gq.at[c])
     for d in outs:

time: 463 us -> 312 us (0.67)
  the two profiles are of different devices: /device:TPU:0 before, /device:TPU:9 now
where the time goes in v2:
time: 312 us; the launch traced here: 307 us
  Pallas kernels  279 us (89%)
  local copies, waits for them, and re-layouts  17 us (5%)
  other arithmetic  5.91 us (2%)
    pallas_call x1, Pallas kernels, fast_device(): pl.pallas_call(layer_kernel, name='layer', out_shape=[jax.ShapeDtypeStruc...  279 us

profile of v2, /device:TPU:9, one launch (start us, length us, event | category | flops | bytes accessed | tf_op | source)
XLA Modules:
  0.0 306.7 jit_solution(10691116327728367055)
XLA Ops:
  0.7 1.0 dynamic_update_slice.6
  1.6 0.8 dynamic_update_slice.7
  2.5 0.6 pad_maximum_fusion.1.refs_4_
  3.1 4.9 %fusion = pred[1408,1536]{1,0:T(32,128)(4,1)S(1)} fusion(s32[1536]{0:T(1024)S(1)} %get-tuple-element.36, s32[1536]{0:T(1024)S(1)} %get-tuple-element.41, s32[1408]{0:T(1024)S(1)} %get-tuple-element.38, s32[1408]{0:T(1024)S(1)} %get-tuple-element.39, s32[1536]{0:T(1024)S(1)} %get-tuple-element.35, s32[1536]{0:T(1024)S(1)} %get-tuple-element.42, ...), kind=kLoop, calls=%fused_computation.2 | loop fusion | flops 15138816 | bytes 2215680 | tf_op jit(solution)/shard_map/and | solution.py:1209
  8.1 0.1 reshape.78
  8.3 1.4 convolution_convert_fusion
  9.8 0.1 reshape.79
  9.9 0.3 copy.42
  10.2 1.0 reshape.80.refs_6_
  11.5 0.3 maximum_bitcast_fusion
  11.8 0.8 reshape.77.refs_5_
  12.6 0.7 pad.9.refs_8_
  13.3 0.6 pad.8.refs_3_
  13.9 279.2 %layer.1 = (bf16[256,1024]{1,0:T(8,128)(2,1)}, bf16[256,1024]{1,0:T(8,128)(2,1)}, bf16[256,1024]{1,0:T(8,128)(2,1)}, bf16[4,32,768]{2,1,0:T(8,128)(2,1)}, bf16[4...) custom-call(bf16[256,1024]{1,0:T(8,128)(2,1)} %refs_0_.1, ...), custom_call_target="tpu_custom_call" | custom-call | tf_op jit(solution)/shard_map/layer/pallas_call | solution.py:1242
  293.2 0.9 constant_dynamic-slice_fusion
  294.1 0.5 slice_bitcast_fusion
  294.6 1.1 reshape.81
  295.7 0.5 copy.39
  296.3 1.6 fusion.15
  297.9 0.8 squeeze.26
  298.7 0.8 squeeze.27
  299.6 0.2 reshape.83
  299.8 0.1 fusion.14
  299.9 0.1 copy.36
  300.0 0.7 squeeze.22
  300.8 0.7 squeeze.23
  301.6 0.7 squeeze.24
  302.3 0.8 slice.36
  303.1 0.8 copy.53
  303.9 0.8 copy.54
  304.7 0.8 copy.55
  305.5 0.7 copy.56
  (50 shorter events, 0.7 us)
Async XLA Ops:
  0.6 7.4 %copy-start.9 = (bf16[32,2816]{1,0:T(8,128)(2,1)S(1)}, bf16[32,2816]{1,0:T(8,128)(2,1)}, u32[]{:S(2)}) copy-start(bf16[32,2816]{1,0:T(8,128)(2,1)} %param.21) | copy-start | bytes 540676
  0.7 7.4 %copy-start.8 = (bf16[32,2816]{1,0:T(8,128)(2,1)S(1)}, bf16[32,2816]{1,0:T(8,128)(2,1)}, u32[]{:S(2)}) copy-start(bf16[32,2816]{1,0:T(8,128)(2,1)} %param.22) | copy-start | bytes 540676
  8.1 1.7 copy-start
  8.3 2.9 copy-start.11
  9.7 1.6 copy-start.12
  9.8 1.7 copy-start.13
  9.8 2.8 copy-start.7
  9.8 3.5 %copy-start.14 = (s32[256]{0:T(256)S(1)}, s32[256]{0:T(256)}, u32[]{:S(2)}) copy-start(s32[256]{0:T(256)} %param.24) | copy-start | bytes 3076
  293.1 3.1 %copy-start.1 = (pred[1408,1536]{1,0:T(32,128)(4,1)S(1)}, pred[1408,1536]{1,0:T(32,128)(4,1)}, u32[]{:S(2)}) copy-start(pred[1408,1536]{1,0:T(32,128)(4,1)} %copy-done) | copy-start | bytes 6488068
  297.8 1.8 copy-start.6
  297.9 4.5 %copy-start.5 = (f32[96,1024]{1,0:T(8,128)S(1)}, f32[96,1024]{1,0:T(8,128)}, u32[]{:S(2)}) copy-start(f32[96,1024]{1,0:T(8,128)} %get-tuple-element.27) | copy-start | bytes 1179652
  298.7 4.4 %copy-start.4 = (bf16[256,1024]{1,0:T(8,128)(2,1)S(1)}, bf16[256,1024]{1,0:T(8,128)(2,1)}, u32[]{:S(2)}) copy-start(bf16[256,1024]{1,0:T(8,128)(2,1)} %get-tuple-element.59) | copy-start | bytes 1572868
  299.8 4.1 %copy-start.3 = (bf16[256,1024]{1,0:T(8,128)(2,1)S(1)}, bf16[256,1024]{1,0:T(8,128)(2,1)}, u32[]{:S(2)}) copy-start(bf16[256,1024]{1,0:T(8,128)(2,1)} %get-tuple-element.60) | copy-start | bytes 1572868
  299.9 4.8 %copy-start.2 = (bf16[256,1024]{1,0:T(8,128)(2,1)S(1)}, bf16[256,1024]{1,0:T(8,128)(2,1)}, u32[]{:S(2)}) copy-start(bf16[256,1024]{1,0:T(8,128)(2,1)} %get-tuple-element.61) | copy-start | bytes 1572868
  301.5 4.0 %copy-start.10 = (f32[32,1024]{1,0:T(8,128)S(1)}, f32[32,1024]{1,0:T(8,128)}, u32[]{:S(2)}) copy-start(f32[32,1024]{1,0:T(8,128)} %get-tuple-element.66) | copy-start | bytes 393220
